TPU v7x, 32 devices: a whole 2x2x4 slice. The times are simulated.
32 devices in a mesh: seq: 8 (over y, x, core), head: 4 (over z).
Axes of the slice: x: 2, y: 2, z: 4, core: 2. Of those that a mesh axis runs over, the one named last changes fastest.
Arguments:
- tokens: bfloat16 [8192, 1024], P(('seq', 'head')), may hold values from -6 to 6
- cotangent: bfloat16 [8192, 1024], P(('seq', 'head')), may hold values from -6 to 6
- image_counts: int32 [8, 9], P('seq'), may hold values from 6 to 896, as said below
- ln1_gain: float32 [1024], replicated, may hold values from 0.1 to 1.9
- ln1_bias: float32 [1024], replicated, may hold values from -3 to 3
- qkv_weight: bfloat16 [1024, 3072], replicated, may hold values from -0.1875 to 0.1875
- query_bias: float32 [1024], replicated, may hold values from -3 to 3
- value_bias: float32 [1024], replicated, may hold values from -3 to 3
- out_weight: bfloat16 [1024, 1024], replicated, may hold values from -0.75 to 0.75
- out_bias: float32 [1024], replicated, may hold values from -3 to 3
- scale_attn: float32 [1024], replicated, may hold values from 0.3 to 3
- ln2_gain: float32 [1024], replicated, may hold values from 0.1 to 1.9
- ln2_bias: float32 [1024], replicated, may hold values from -3 to 3
- up_weight: bfloat16 [1024, 4096], replicated, may hold values from -0.1875 to 0.1875
- up_bias: float32 [4096], replicated, may hold values from -3 to 3
- down_weight: bfloat16 [4096, 1024], replicated, may hold values from -0.09375 to 0.09375
- down_bias: float32 [1024], replicated, may hold values from -3 to 3
- scale_mlp: float32 [1024], replicated, may hold values from 0.3 to 3
Outputs:
- output: bfloat16 [8192, 1024], P(('seq', 'head'))
- tokens_grad: float32 [8192, 1024], P(('seq', 'head'))
- ln1_gain_grad: float32 [1024], P('seq')
- ln1_bias_grad: float32 [1024], P('seq')
- qkv_weight_grad: float32 [1024, 3072], P('seq')
- query_bias_grad: float32 [1024], P('seq')
- value_bias_grad: float32 [1024], P('seq')
- out_weight_grad: float32 [1024, 1024], P('seq')
- out_bias_grad: float32 [1024], P('seq')
- scale_attn_grad: float32 [1024], P('seq')
- ln2_gain_grad: float32 [1024], P('seq')
- ln2_bias_grad: float32 [1024], P('seq')
- up_weight_grad: float32 [1024, 4096], P('seq')
- up_bias_grad: float32 [4096], P('seq')
- down_weight_grad: float32 [4096, 1024], P('seq')
- down_bias_grad: float32 [1024], P('seq')
- scale_mlp_grad: float32 [1024], P('seq')
Inputs may be any that keep to these rules, and one draw needn't show every extreme that they name: `image_counts`: row g lists the token counts of group g's 9 images in order and sums to 1024; image 4 (from 0) is the group's largest and holds at least 640 tokens; every image has 5 special tokens and one patch or more.
All inputs are finite; a program needn't handle non-finite values.
Results may differ from a plain program's by a relative error of at most 0.015.
Values may be sent and summed in bfloat16 or wider, within the bound.
No kernel may reach another device: no remote copies, remote signals or barrier semaphores. Data moves between devices by JAX's collectives and lax.ppermute only.
A program may use at most 192 MiB of HBM per device.

v0:
```python
import jax
import jax.numpy as jnp
from jax import lax
from jax.sharding import PartitionSpec as P

HEAD_DIM = 64


EPSILON = 1e-06
NEGATIVE = -1e30


def layer_norm(values, scale_gain, shift_bias):
    average = jnp.mean(values, -1, keepdims=True)
    centered = values - average
    inverse = lax.rsqrt(jnp.mean(centered * centered, -1, keepdims=True) + EPSILON)
    unit_rows = centered * inverse
    return (unit_rows * scale_gain + shift_bias, unit_rows, inverse)


def norm_back(grad_normed, unit_rows, inverse, scale_gain):
    grad_unit = grad_normed * scale_gain
    first_term = jnp.mean(grad_unit, -1, keepdims=True)
    second_term = jnp.mean(grad_unit * unit_rows, -1, keepdims=True)
    grad_input = inverse * (grad_unit - first_term - unit_rows * second_term)
    return (grad_input, jnp.sum(grad_normed * unit_rows, 0), jnp.sum(grad_normed, 0))


def contract_rows(left, right):
    return lax.dot_general(
        left, right, (((0,), (0,)), ((), ())), preferred_element_type=jnp.float32
    )


def times_transpose(left, right):
    return lax.dot_general(
        left, right, (((1,), (1,)), ((), ())), preferred_element_type=jnp.float32
    )


def gelu_exact(values):
    return jax.nn.gelu(values, approximate=False)


def image_index(counts_row, length):
    boundary = jnp.cumsum(counts_row)
    places = jnp.arange(length, dtype=jnp.int32)
    return jnp.sum((places[:, None] >= boundary[None, :]).astype(jnp.int32), 1)


def block_scores(query_rows, query_labels, keys, labels, factor):
    scores = (
        jnp.einsum("qhd,khd->hqk", query_rows, keys, preferred_element_type=jnp.float32) * factor
    )
    return jnp.where((query_labels[:, None] == labels[None, :])[None], scores, NEGATIVE)


def attend(queries, keys, values, labels):
    length = queries.shape[0]
    block = min(512, length)
    factor = queries.shape[2] ** (-0.5)

    def one_block(number):
        start = number * block
        query_rows = lax.dynamic_slice_in_dim(queries, start, block, 0)
        query_labels = lax.dynamic_slice_in_dim(labels, start, block, 0)
        scores = block_scores(query_rows, query_labels, keys, labels, factor)
        highest = jnp.max(scores, -1, keepdims=True)
        logsum = highest + jnp.log(jnp.sum(jnp.exp(scores - highest), -1, keepdims=True))
        probs = jnp.exp(scores - logsum).astype(jnp.bfloat16)
        mixed = jnp.einsum("hqk,khd->qhd", probs, values, preferred_element_type=jnp.float32)
        return (mixed.astype(jnp.bfloat16), logsum[..., 0])

    mixed, logsum = lax.map(one_block, jnp.arange(length // block, dtype=jnp.int32))
    return (mixed.reshape(queries.shape), logsum)


def attend_back(queries, keys, values, labels, logsum, grad_mixed):
    length = queries.shape[0]
    block = min(512, length)
    factor = queries.shape[2] ** (-0.5)

    def one_block(carry, number):
        grad_keys, grad_values = carry
        start = number * block
        query_rows = lax.dynamic_slice_in_dim(queries, start, block, 0)
        query_labels = lax.dynamic_slice_in_dim(labels, start, block, 0)
        grad_rows = lax.dynamic_slice_in_dim(grad_mixed, start, block, 0)
        scores = block_scores(query_rows, query_labels, keys, labels, factor)
        probs_full = jnp.exp(scores - logsum[number][..., None])
        probs = probs_full.astype(jnp.bfloat16)
        grad_probs = jnp.einsum(
            "qhd,khd->hqk", grad_rows, values, preferred_element_type=jnp.float32
        )
        balance = jnp.sum(probs_full * grad_probs, -1, keepdims=True)
        grad_scores = (probs_full * (grad_probs - balance)).astype(jnp.bfloat16)
        grad_query = (
            jnp.einsum("hqk,khd->qhd", grad_scores, keys, preferred_element_type=jnp.float32)
            * factor
        )
        grad_keys = (
            grad_keys
            + jnp.einsum(
                "hqk,qhd->khd", grad_scores, query_rows, preferred_element_type=jnp.float32
            )
            * factor
        )
        grad_values = grad_values + jnp.einsum(
            "hqk,qhd->khd", probs, grad_rows, preferred_element_type=jnp.float32
        )
        return ((grad_keys, grad_values), grad_query)

    start_carry = (jnp.zeros(keys.shape, jnp.float32), jnp.zeros(values.shape, jnp.float32))
    (grad_keys, grad_values), grad_queries = lax.scan(
        one_block, start_carry, jnp.arange(length // block, dtype=jnp.int32)
    )
    return (grad_queries.reshape(queries.shape), grad_keys, grad_values)


def body(
    tokens,
    cotangent,
    image_counts,
    ln1_gain,
    ln1_bias,
    qkv_weight,
    query_bias,
    value_bias,
    out_weight,
    out_bias,
    scale_attn,
    ln2_gain,
    ln2_bias,
    up_weight,
    up_bias,
    down_weight,
    down_bias,
    scale_mlp,
):
    rows_here, width = tokens.shape
    head_devices = lax.axis_size("head")
    local_width = width // head_devices
    local_heads = local_width // HEAD_DIM
    length = rows_here * head_devices
    labels = image_index(image_counts[0], length)
    qkv_bias = jnp.concatenate([query_bias, jnp.zeros_like(query_bias), value_bias])
    inputs = tokens.astype(jnp.float32)

    def forward(again):
        normed1, unit1, inverse1 = layer_norm(inputs, ln1_gain, ln1_bias)
        normed1 = normed1.astype(jnp.bfloat16)
        projected = jnp.dot(normed1, qkv_weight, preferred_element_type=jnp.float32) + qkv_bias
        projected = projected.astype(jnp.bfloat16).reshape(rows_here, 3, width)
        if again:
            spread = lax.all_to_all(projected, "head", split_axis=2, concat_axis=0, tiled=True)
        else:
            spread = lax.all_to_all(projected, "head", split_axis=2, concat_axis=0, tiled=True)
        queries = spread[:, 0].reshape(length, local_heads, HEAD_DIM)
        keys = spread[:, 1].reshape(length, local_heads, HEAD_DIM)
        values = spread[:, 2].reshape(length, local_heads, HEAD_DIM)
        head_mixed, logsum = attend(queries, keys, values, labels)
        flat_mixed = head_mixed.reshape(length, local_width)
        if again:
            mixed = lax.all_to_all(flat_mixed, "head", split_axis=0, concat_axis=1, tiled=True)
        else:
            mixed = lax.all_to_all(flat_mixed, "head", split_axis=0, concat_axis=1, tiled=True)
        attended = jnp.dot(mixed, out_weight, preferred_element_type=jnp.float32) + out_bias
        middle = inputs + scale_attn * attended
        normed2, unit2, inverse2 = layer_norm(middle, ln2_gain, ln2_bias)
        normed2 = normed2.astype(jnp.bfloat16)
        upward = jnp.dot(normed2, up_weight, preferred_element_type=jnp.float32) + up_bias
        active = gelu_exact(upward).astype(jnp.bfloat16)
        downward = jnp.dot(active, down_weight, preferred_element_type=jnp.float32) + down_bias
        result = (middle + scale_mlp * downward).astype(jnp.bfloat16)
        saved = (
            unit1,
            inverse1,
            normed1,
            queries,
            keys,
            values,
            logsum,
            mixed,
            attended,
            unit2,
            inverse2,
            normed2,
            upward,
            active,
            downward,
        )
        return (result, saved)

    output = forward(False)[0]
    saved = forward(True)[1]
    (
        unit1,
        inverse1,
        normed1,
        queries,
        keys,
        values,
        logsum,
        mixed,
        attended,
        unit2,
        inverse2,
        normed2,
        upward,
        active,
        downward,
    ) = saved
    grad_output = cotangent.astype(jnp.float32)
    scale_mlp_grad = jnp.sum(grad_output * downward, 0)
    grad_down = (scale_mlp * grad_output).astype(jnp.bfloat16)
    down_bias_grad = jnp.sum(grad_down, 0, dtype=jnp.float32)
    down_weight_grad = contract_rows(active, grad_down)
    grad_active = times_transpose(grad_down, down_weight)
    grad_up = jax.vjp(gelu_exact, upward)[1](grad_active)[0].astype(jnp.bfloat16)
    up_bias_grad = jnp.sum(grad_up, 0, dtype=jnp.float32)
    up_weight_grad = contract_rows(normed2, grad_up)
    grad_normed2 = times_transpose(grad_up, up_weight)
    grad_middle_norm, ln2_gain_grad, ln2_bias_grad = norm_back(
        grad_normed2, unit2, inverse2, ln2_gain
    )
    grad_middle = grad_output + grad_middle_norm
    scale_attn_grad = jnp.sum(grad_middle * attended, 0)
    grad_attended = (scale_attn * grad_middle).astype(jnp.bfloat16)
    out_bias_grad = jnp.sum(grad_attended, 0, dtype=jnp.float32)
    out_weight_grad = contract_rows(mixed, grad_attended)
    grad_mixed = times_transpose(grad_attended, out_weight).astype(jnp.bfloat16)
    head_grad = lax.all_to_all(grad_mixed, "head", split_axis=1, concat_axis=0, tiled=True).reshape(
        length, local_heads, HEAD_DIM
    )
    grad_queries, grad_keys, grad_values = attend_back(
        queries, keys, values, labels, logsum, head_grad
    )
    stacked = jnp.stack(
        [
            grad_queries.reshape(length, local_width),
            grad_keys.reshape(length, local_width),
            grad_values.reshape(length, local_width),
        ],
        1,
    ).astype(jnp.bfloat16)
    grad_qkv = lax.all_to_all(stacked, "head", split_axis=0, concat_axis=2, tiled=True).reshape(
        rows_here, 3 * width
    )
    query_bias_grad = jnp.sum(grad_qkv[:, :width], 0, dtype=jnp.float32)
    value_bias_grad = jnp.sum(grad_qkv[:, 2 * width :], 0, dtype=jnp.float32)
    qkv_weight_grad = contract_rows(normed1, grad_qkv)
    grad_normed1 = times_transpose(grad_qkv, qkv_weight)
    grad_front, ln1_gain_grad, ln1_bias_grad = norm_back(grad_normed1, unit1, inverse1, ln1_gain)
    tokens_grad = grad_middle + grad_front
    (
        ln1_gain_grad,
        ln1_bias_grad,
        qkv_weight_grad,
        query_bias_grad,
        value_bias_grad,
        out_weight_grad,
        out_bias_grad,
        scale_attn_grad,
        ln2_gain_grad,
        ln2_bias_grad,
        up_weight_grad,
        up_bias_grad,
        down_weight_grad,
        down_bias_grad,
        scale_mlp_grad,
    ) = (
        lax.psum_scatter(
            ln1_gain_grad.astype(jnp.bfloat16), "seq", scatter_dimension=0, tiled=True
        ).astype(jnp.float32),
        lax.psum_scatter(
            ln1_bias_grad.astype(jnp.bfloat16), "seq", scatter_dimension=0, tiled=True
        ).astype(jnp.float32),
        lax.psum_scatter(
            qkv_weight_grad.astype(jnp.bfloat16), "seq", scatter_dimension=0, tiled=True
        ).astype(jnp.float32),
        lax.psum_scatter(
            query_bias_grad.astype(jnp.bfloat16), "seq", scatter_dimension=0, tiled=True
        ).astype(jnp.float32),
        lax.psum_scatter(
            value_bias_grad.astype(jnp.bfloat16), "seq", scatter_dimension=0, tiled=True
        ).astype(jnp.float32),
        lax.psum_scatter(
            out_weight_grad.astype(jnp.bfloat16), "seq", scatter_dimension=0, tiled=True
        ).astype(jnp.float32),
        lax.psum_scatter(
            out_bias_grad.astype(jnp.bfloat16), "seq", scatter_dimension=0, tiled=True
        ).astype(jnp.float32),
        lax.psum_scatter(
            scale_attn_grad.astype(jnp.bfloat16), "seq", scatter_dimension=0, tiled=True
        ).astype(jnp.float32),
        lax.psum_scatter(
            ln2_gain_grad.astype(jnp.bfloat16), "seq", scatter_dimension=0, tiled=True
        ).astype(jnp.float32),
        lax.psum_scatter(
            ln2_bias_grad.astype(jnp.bfloat16), "seq", scatter_dimension=0, tiled=True
        ).astype(jnp.float32),
        lax.psum_scatter(
            up_weight_grad.astype(jnp.bfloat16), "seq", scatter_dimension=0, tiled=True
        ).astype(jnp.float32),
        lax.psum_scatter(
            up_bias_grad.astype(jnp.bfloat16), "seq", scatter_dimension=0, tiled=True
        ).astype(jnp.float32),
        lax.psum_scatter(
            down_weight_grad.astype(jnp.bfloat16), "seq", scatter_dimension=0, tiled=True
        ).astype(jnp.float32),
        lax.psum_scatter(
            down_bias_grad.astype(jnp.bfloat16), "seq", scatter_dimension=0, tiled=True
        ).astype(jnp.float32),
        lax.psum_scatter(
            scale_mlp_grad.astype(jnp.bfloat16), "seq", scatter_dimension=0, tiled=True
        ).astype(jnp.float32),
    )
    (
        ln1_gain_grad,
        ln1_bias_grad,
        qkv_weight_grad,
        query_bias_grad,
        value_bias_grad,
        out_weight_grad,
        out_bias_grad,
        scale_attn_grad,
        ln2_gain_grad,
        ln2_bias_grad,
        up_weight_grad,
        up_bias_grad,
        down_weight_grad,
        down_bias_grad,
        scale_mlp_grad,
    ) = lax.psum(
        (
            ln1_gain_grad,
            ln1_bias_grad,
            qkv_weight_grad,
            query_bias_grad,
            value_bias_grad,
            out_weight_grad,
            out_bias_grad,
            scale_attn_grad,
            ln2_gain_grad,
            ln2_bias_grad,
            up_weight_grad,
            up_bias_grad,
            down_weight_grad,
            down_bias_grad,
            scale_mlp_grad,
        ),
        "head",
    )
    return (
        output,
        tokens_grad,
        ln1_gain_grad,
        ln1_bias_grad,
        qkv_weight_grad,
        query_bias_grad,
        value_bias_grad,
        out_weight_grad,
        out_bias_grad,
        scale_attn_grad,
        ln2_gain_grad,
        ln2_bias_grad,
        up_weight_grad,
        up_bias_grad,
        down_weight_grad,
        down_bias_grad,
        scale_mlp_grad,
    )


def solution(mesh):
    in_specs = (
        P(("seq", "head"), None),
        P(("seq", "head"), None),
        P("seq", None),
        P(),
        P(),
        P(),
        P(),
        P(),
        P(),
        P(),
        P(),
        P(),
        P(),
        P(),
        P(),
        P(),
        P(),
        P(),
    )
    out_specs = (
        P(("seq", "head"), None),
        P(("seq", "head"), None),
        P("seq"),
        P("seq"),
        P("seq", None),
        P("seq"),
        P("seq"),
        P("seq", None),
        P("seq"),
        P("seq"),
        P("seq"),
        P("seq"),
        P("seq", None),
        P("seq"),
        P("seq", None),
        P("seq"),
        P("seq"),
    )
    return jax.shard_map(body, mesh=mesh, in_specs=in_specs, out_specs=out_specs, check_vma=False)
```

profile of v0, /device:TPU:0, one launch (start us, length us, event | category | flops | bytes accessed | tf_op | source)
XLA Modules:
  0.0 704.4 jit_solution(8909886217677611104)
XLA Ops:
  10.6 6.1 fusion.64
  16.7 2.6 copy.107
  19.3 4.1 copy.108
  23.3 6.3 all-to-all-start
  30.0 48.0 %all-to-all-done = bf16[256,3,1024]{0,1,2:T(4,128)(2,1)} async-done(((bf16[256,3,1024]{0,1,2:T(4,128)(2,1)}), bf16[256,3,1024]{0,1,2:T(4,128)(2,1)}, u32[]{:S(2)}, u32[]{:S(2)}) %all-to-all-start) | async-done | bytes 1572896 | tf_op jit(solution)/shard_map/all_to_all | solution.py:157
  78.0 3.0 copy.109
  80.9 2.6 copy.110
  83.5 2.3 fusion.176
  89.8 19.7 %while.38 = (s32[]{:T(128)}, bf16[2,512,4,64]{1,3,2,0:T(8,128)(2,1)}, f32[2,4,512]{2,1,0:T(4,128)S(1)}, s32[2]{0:T(128)S(1)}, s32[1024]{0:T(1024)S(1)}, /*index=...) while((s32[]{:T(128)}, ...), condition=%wide.region_13.14_spmd, body=%wide.region_10.13_spmd.sunk | while | flops 560592896 | bytes 35203344 | solution.py:74
  91.5 2.6 fusion.237
  94.2 2.3 exponential_reduce_fusion.5
  96.6 2.3 fusion.238
  101.4 2.6 fusion.237
  104.0 2.3 exponential_reduce_fusion.5
  106.4 2.3 fusion.238
  109.5 2.4 copy.116
  112.0 2.9 all_to_all.77
  116.0 16.6 %all_to_all.92 = bf16[4,256,256]{1,2,0:T(8,128)(2,1)S(1)} all-to-all(bf16[4,256,256]{1,2,0:T(8,128)(2,1)S(1)} %copy.117), channel_id=1, replica_groups=mesh['seq'=8,'head'=4] {'head'}, dimensions={0} | all-to-all | bytes 1048576 | tf_op jit(solution)/shard_map/all_to_all | solution.py:164
  133.8 15.5 %multiply_convert_fusion.1 = (bf16[256,4096]{1,0:T(8,128)(2,1)}, f32[256,4096]{1,0:T(8,128)S(1)}, f32[256,4096]{1,0:T(8,128)}) fusion(f32[4096]{0:T(1024)S(1)} %copy-done.39, bf16[1024,4096]{1,0:T(8,128)(2,1)} %param.37, f32[256,1024]{1,0:T(8,128)S(1)} %get-tuple-element.332, f32[256]{0:T(256)S(1)} %add_rsqrt_fusion, f32[256]{0:T(256)S(1)} %broadcast_multiply_fusion.4, ...), kind=kOutput, calls=%fused_computation.72 | convolution fusion | flops 2218000384 | bytes 19949568 | tf_op jit(solution)/shard_map/dot_general | solution.py:171
  149.2 11.8 %fusion.178 = (bf16[4096]{0:T(1024)(128)(2,1)}, bf16[256,4096]{1,0:T(8,128)(2,1)S(1)}) fusion(f32[256,4096]{1,0:T(8,128)S(1)} %get-tuple-element.326, f32[256,4096]{1,0:T(8,128)} %get-tuple-element.345, bf16[4096,1024]{1,0:T(8,128)(2,1)} %param.39, bf16[256,1024]{1,0:T(8,128)(2,1)S(1)} %copy-done.9, f32[1024]{0:T(1024)S(1)} %copy-done.31), kind=kOutput, calls=%fused_computation.248 | convolution fusion | flops 2163994624 | bytes 19410944 | tf_op jit(solution)/shard_map/dot_general | solution.py:36
  161.0 7.7 %multiply_reduce_fusion.1 = (bf16[1024]{0:T(1024)(128)(2,1)}, f32[256]{0:T(256)S(1)}, f32[256]{0:T(256)S(1)}, bf16[1024]{0:T(1024)(128)(2,1)}, f32[256,1024]{1,0:T(8,128)S(1)}) fusion(f32[256,1024]{1,0:T(8,128)S(1)} %get-tuple-element.332, f32[256]{0:T(256)S(1)} %add_rsqrt_fusion, f32[256]{0:T(256)S(1)} %broadcast_multiply_fusion.4, ...), kind=kOutput, calls=%fused_computation.170 | convolution fusion | flops 2149840384 | bytes 12595200 | tf_op jit(solution)/shard_map/dot_general | solution.py:36
  171.6 2.1 convolution_convert_fusion.3
  173.7 7.7 %convolution_convert_fusion.1 = bf16[1024,4096]{1,0:T(8,128)(2,1)} fusion(bf16[256,4096]{1,0:T(8,128)(2,1)} %copy-done.13, f32[256,1024]{1,0:T(8,128)} %copy-done.4, f32[256]{0:T(256)S(1)} %add_rsqrt_fusion, f32[256]{0:T(256)S(1)} %broadcast_multiply_fusion.4, f32[1024]{0:T(1024)S(1)} %copy-done.27, f32[1024]{0:T(1024)S(1)} %copy-done.22), kind=kOutput, calls=%fused_computation.62 | convolution fusion | flops 2152988672 | bytes 11544576 | tf_op jit(solution)/shard_map/dot_general | solution.py:30
  182.9 3.5 all-to-all-start.3
  186.5 13.4 %all-to-all-done.3 = bf16[256,4,256]{2,0,1:T(8,128)(2,1)S(1)} async-done(((bf16[256,4,256]{2,0,1:T(8,128)(2,1)}), bf16[256,4,256]{2,0,1:T(8,128)(2,1)S(1)}, u32[]{:S(2)}, u32[]{:S(2)}) %all-to-all-start.3) | async-done | bytes 524320 | tf_op jit(solution)/shard_map/all_to_all | solution.py:232
  201.0 2.2 reshape.268
  203.2 67.5 %while.39 = (s32[]{:T(128)}, f32[1024,4,64]{0,2,1:T(8,128)}, f32[1024,4,64]{0,2,1:T(8,128)}, bf16[2,512,4,64]{1,3,2,0:T(8,128)(2,1)}, s32[2]{0:T(128)S(1)}, /*in...) while((s32[]{:T(128)}, f32[1024,4,64]{0,2,1:T(8,128)}, ...), condition=%wide.region_20.21_spmd.clone, body=%wide.region_18.20_spmd.clone.sunk | while | flops 1375598592 | bytes 120654272 | solution.py:114
  204.9 5.5 fusion.248
  212.8 6.9 multiply_reduce_fusion.9
  219.7 3.7 multiply_convert_fusion.5
  223.4 4.4 fusion.249
  230.7 6.8 fusion.250
  238.7 5.7 fusion.248
  246.8 7.1 %multiply_reduce_fusion.9 = (f32[4,512]{1,0:T(4,128)S(1)}, f32[4,512,1024]{2,1,0:T(8,128)S(1)}) fusion(f32[4,512,1024]{2,1,0:T(8,128)} %fusion.248, f32[4,512]{1,0:T(4,128)S(1)} %dynamic-slice_bitcast_fusion.2, pred[512,1024]{1,0:T(8,128)(4,1)S(1)} %broadcast_compare_fusion.8, bf16[1024,4,64]{0,2,1:T(8,128)(2,1)} %get-tuple-element.638, ...), kind=kOutput, calls=%fused_computation.34.clone.1 | convolution fusion | flops 278919168 | bytes 18104324 | tf_op jit(solution)/shard_map/while/body/eval_jaxpr/qhd,khd->hqk/dot_general | solution.py:92
  254.0 3.7 multiply_convert_fusion.5
  257.7 4.6 fusion.249
  264.5 6.2 fusion.250
  270.7 1.6 copy.120
  276.3 2.4 pad_maximum_fusion
  278.6 4.1 copy.121
  282.8 52.0 %all_to_all.93 = bf16[1024,3,256]{2,1,0:T(4,128)(2,1)S(1)} all-to-all(bf16[1024,3,256]{2,1,0:T(4,128)(2,1)} %copy.121), channel_id=1, replica_groups=mesh['seq'=8,'head'=4] {'head'}, dimensions={0} | all-to-all | bytes 3145728 | tf_op jit(solution)/shard_map/all_to_all | solution.py:246
  336.2 2.6 copy.123
  338.8 6.1 convolution_convert_fusion.2
  345.0 7.9 %convolution_convert_fusion = bf16[4096,1024]{1,0:T(8,128)(2,1)} fusion(bf16[256,4096]{1,0:T(8,128)(2,1)} %get-tuple-element.325, bf16[256,1024]{1,0:T(8,128)(2,1)} %param.25, f32[1024]{0:T(1024)S(1)} %copy-done.31), kind=kOutput, calls=%fused_computation.61 | convolution fusion | flops 2152464384 | bytes 11014144 | tf_op jit(solution)/shard_map/dot_general | solution.py:30
  353.8 19.3 %while.37 = (s32[]{:T(128)}, bf16[2,512,4,64]{1,3,2,0:T(8,128)(2,1)}, s32[2]{0:T(128)S(1)}, s32[1024]{0:T(1024)S(1)}, bf16[1024,4,64]{0,2,1:T(8,128)(2,1)}, /*in...) while((s32[]{:T(128)}, ...), condition=%wide.region_7.8_spmd, body=%wide.region_4.7_spmd.sunk | while | flops 560592896 | bytes 31001292 | solution.py:74
  355.5 2.7 fusion.233
  358.1 2.3 exponential_reduce_fusion.4
  360.5 3.0 fusion.234
  365.2 2.6 fusion.233
  367.8 2.3 exponential_reduce_fusion.4
  370.2 3.0 fusion.234
  373.2 2.4 copy.114
  375.6 2.9 all_to_all.73
  378.5 1.9 copy.115
  380.4 4.3 all-to-all-start.1
  386.8 12.0 %all-to-all-done.1 = bf16[4,256,256]{1,2,0:T(8,128)(2,1)} async-done(((bf16[4,256,256]{1,2,0:T(8,128)(2,1)}), bf16[4,256,256]{1,2,0:T(8,128)(2,1)}, u32[]{:S(2)}, u32[]{:S(2)}) %all-to-all-start.1) | async-done | bytes 524320 | tf_op jit(solution)/shard_map/all_to_all | solution.py:166
  398.8 2.0 fusion.177
  402.1 5.9 fusion.117
  408.1 20.3 %fusion.108 = bf16[256,1024]{1,0:T(8,128)(2,1)} fusion(f32[256,1024]{1,0:T(8,128)} %copy-done.11, bf16[4096,1024]{1,0:T(8,128)(2,1)} %param.39, bf16[1024,4096]{1,0:T(8,128)(2,1)} %param.37, f32[4096]{0:T(1024)S(1)} %copy-done.40, f32[1024]{0:T(1024)S(1)} %copy-done.41, f32[1024]{0:T(1024)S(1)} %copy-done.28, f32[1024]{0:T(1024)S(1)} %copy-done.23, ...), kind=kOutput, calls=%fused_computation.153 | convolution fusion | flops 4366532608 | bytes 18384896 | tf_op jit(solution)/shard_map/dot_general | solution.py:173
  430.0 6.3 fusion.124
  436.3 23.2 %all-reduce.12 = (bf16[1024]{0:T(1024)(128)(2,1)S(1)}, bf16[1024]{0:T(1024)(128)(2,1)S(1)}, bf16[1024]{0:T(1024)(128)(2,1)S(1)}, bf16[1024]{0:T(1024)(128)(2,1)S...) all-reduce(bf16[1024]{0:T(1024)(128)(2,1)S(1)} %get-tuple-element.2, ...), channel_id=2, replica_groups=mesh['seq'=8,'head'=4] {'seq'}, use_global_device_ids=true, to_apply=%region_24.25.clone | all-reduce | flops 14336 | bytes 57344
  460.4 2.9 fusion.123
  463.3 17.4 %reduce-scatter.11.cloned.1.call-done = bf16[512,1024]{1,0:T(8,128)(2,1)} async-done(((bf16[4096,1024]{1,0:T(8,128)(2,1)}), bf16[512,1024]{1,0:T(8,128)(2,1)}) %reduce-scatter.11.cloned.1.call-update) | async-done | bytes 1048592 | tf_op jit(solution)/shard_map/reduce_scatter | solution.py:308
  480.7 216.7 %all-reduce.14 = (f32[128]{0:T(128)}, f32[128]{0:T(128)}, f32[128,3072]{1,0:T(8,128)}, f32[128]{0:T(128)}, f32[128]{0:T(128)}, /*index=5*/f32[128,1024]{1,0:T(8,...) all-reduce(f32[128]{0:T(128)S(1)} %dynamic-slice_convert_fusion.10,, ...), channel_id=1, replica_groups=mesh['seq'=8,'head'=4] {'head'}, use_global_device_ids=true, to_apply=%region_25.26 | all-reduce | flops 1574656 | bytes 9451520 | tf_op jit(solution)/shard_map/psum | solution.py:334
  (205 shorter events, 39.2 us)
Async XLA Ops:
  7.2 125.4 %copy-start = (bf16[1024,1024]{1,0:T(8,128)(2,1)S(1)}, bf16[1024,1024]{1,0:T(8,128)(2,1)}, u32[]{:S(2)}) copy-start(bf16[1024,1024]{1,0:T(8,128)(2,1)} %param.32) | copy-start | bytes 6291460
  8.5 8.1 %copy-start.29 = (f32[256]{0:T(256)}, f32[256]{0:T(256)S(1)}, u32[]{:S(2)}) copy-start(f32[256]{0:T(256)S(1)} %broadcast_multiply_fusion.6) | copy-start | bytes 3076
  9.9 6.8 copy-start.32
  19.3 10.4 %copy-start.42 = (s32[1,9]{1,0:T(1,128)S(1)}, s32[1,9]{1,0:T(1,128)}, u32[]{:S(2)}) copy-start(s32[1,9]{1,0:T(1,128)} %param.26) | copy-start | bytes 112
  23.3 54.6 %all-to-all-start = ((bf16[256,3,1024]{0,1,2:T(4,128)(2,1)}), bf16[256,3,1024]{0,1,2:T(4,128)(2,1)}, u32[]{:S(2)}, u32[]{:S(2)}) async-start(bf16[256,3,1024]{0,1,2:T(4,128)(2,1)} %copy.108), calls=%async_computation | async-start | bytes 4194304 | tf_op jit(solution)/shard_map/all_to_all | solution.py:157
  29.7 398.7 %reduce-scatter.7.cloned.1.call-start = ((), (), s32[]{:S(2)}) async-start(), calls=%async_computation.10 | async-start | bytes 2359296 | tf_op jit(solution)/shard_map/reduce_scatter | solution.py:287
  94.2 2.4 copy-start.5
  94.2 2.4 copy-start.14
  98.9 0.8 copy-start.15
  104.0 2.4 copy-start.5
  104.0 2.4 copy-start.14
  108.7 0.8 copy-start.15
  109.5 23.0 %copy-start.2 = (bf16[256,1024]{1,0:T(8,128)(2,1)S(1)}, bf16[256,1024]{1,0:T(8,128)(2,1)}, u32[]{:S(2)}) copy-start(bf16[256,1024]{1,0:T(8,128)(2,1)} %param.24) | copy-start | bytes 1572868
  109.5 23.0 %copy-start.19 = (f32[1024]{0:T(1024)S(1)}, f32[1024]{0:T(1024)}, u32[]{:S(2)}) copy-start(f32[1024]{0:T(1024)} %param.34) | copy-start | bytes 12292
  109.5 23.0 %copy-start.25 = (f32[1024]{0:T(1024)S(1)}, f32[1024]{0:T(1024)}, u32[]{:S(2)}) copy-start(f32[1024]{0:T(1024)} %param.33) | copy-start | bytes 12292
  114.8 18.9 %copy-start.22 = (f32[1024]{0:T(1024)S(1)}, f32[1024]{0:T(1024)}, u32[]{:S(2)}) copy-start(f32[1024]{0:T(1024)} %param.35) | copy-start | bytes 12292
  114.8 18.9 %copy-start.27 = (f32[1024]{0:T(1024)S(1)}, f32[1024]{0:T(1024)}, u32[]{:S(2)}) copy-start(f32[1024]{0:T(1024)} %param.36) | copy-start | bytes 12292
  114.8 18.9 %copy-start.39 = (f32[4096]{0:T(1024)S(1)}, f32[4096]{0:T(1024)}, u32[]{:S(2)}) copy-start(f32[4096]{0:T(1024)} %param.38) | copy-start | bytes 49156
  133.4 35.3 %copy-start.4 = (f32[256,1024]{1,0:T(8,128)}, f32[256,1024]{1,0:T(8,128)S(1)}, u32[]{:S(2)}) copy-start(f32[256,1024]{1,0:T(8,128)S(1)} %get-tuple-element.332) | copy-start | bytes 3145732
  133.7 15.5 %copy-start.9 = (bf16[256,1024]{1,0:T(8,128)(2,1)S(1)}, bf16[256,1024]{1,0:T(8,128)(2,1)}, u32[]{:S(2)}) copy-start(bf16[256,1024]{1,0:T(8,128)(2,1)} %param.25) | copy-start | bytes 1572868
  133.8 15.5 %copy-start.31 = (f32[1024]{0:T(1024)S(1)}, f32[1024]{0:T(1024)}, u32[]{:S(2)}) copy-start(f32[1024]{0:T(1024)} %param.41) | copy-start | bytes 12292
  161.0 7.7 %copy-start.13 = (bf16[256,4096]{1,0:T(8,128)(2,1)}, bf16[256,4096]{1,0:T(8,128)(2,1)S(1)}, u32[]{:S(2)}) copy-start(bf16[256,4096]{1,0:T(8,128)(2,1)S(1)} %get-tuple-element.349) | copy-start | bytes 6291460
  169.8 1.0 copy-start.7
  173.6 289.7 %reduce-scatter.9.cloned.1.call-start = ((), (), s32[]{:S(2)}) async-start(), calls=%async_computation.11 | async-start | bytes 9437184 | tf_op jit(solution)/shard_map/reduce_scatter | solution.py:302
  182.9 17.0 %all-to-all-start.3 = ((bf16[256,4,256]{2,0,1:T(8,128)(2,1)}), bf16[256,4,256]{2,0,1:T(8,128)(2,1)S(1)}, u32[]{:S(2)}, u32[]{:S(2)}) async-start(bf16[256,4,256]{2,0,1:T(8,128)(2,1)} %bitcast.152), calls=%async_computation.3 | async-start | bytes 1048576 | tf_op jit(solution)/shard_map/all_to_all | solution.py:232
  186.4 276.9 %reduce-scatter.5.cloned.1.call-start = ((), (), s32[]{:S(2)}) async-start(), calls=%async_computation.9 | async-start | bytes 7077888 | tf_op jit(solution)/shard_map/reduce_scatter | solution.py:278
  212.7 7.0 slice-start
  212.7 7.0 slice-start.1
  223.4 4.9 copy-start.1
  223.4 5.1 copy-start.16
  227.8 2.9 copy-start.8
  229.9 0.8 copy-start.17
  246.8 7.2 %slice-start = ((s8[8388608]{0:T(1024)(128)(4,1)}), s8[4194304]{0:T(1024)(128)(4,1)S(1)}, s32[]{:S(2)}) async-start(s8[8388608]{0:T(1024)(128)(4,1)} %bitcast.138), calls=%async_computation.13 | async-start | bytes 8388608 | tf_op jit(solution)/shard_map/while
  246.8 7.2 %slice-start.1 = ((s8[8388608]{0:T(1024)(128)(4,1)}), s8[4194304]{0:T(1024)(128)(4,1)S(1)}, s32[]{:S(2)}) async-start(s8[8388608]{0:T(1024)(128)(4,1)} %bitcast.138), calls=%async_computation.14 | async-start | bytes 8388608 | tf_op jit(solution)/shard_map/while
  257.7 4.6 copy-start.1
  257.7 4.6 copy-start.16
  262.3 2.2 copy-start.8
  263.7 0.8 copy-start.17
  334.8 4.0 copy-start.3
  334.8 4.0 copy-start.21
  334.8 4.0 copy-start.24
  334.8 4.0 copy-start.30
  334.8 4.0 copy-start.33
  345.0 135.7 %reduce-scatter.11.cloned.1.call-start = ((), (), s32[]{:S(2)}) async-start(), calls=%async_computation.12 | async-start | bytes 9437184 | tf_op jit(solution)/shard_map/reduce_scatter | solution.py:308
  358.1 2.4 copy-start.6
  367.8 2.4 copy-start.6
  373.1 11.6 %copy-start.43 = (u32[32]{0:T(128)S(1)}, u32[32]{0:T(128)}, u32[]{:S(2)}) copy-start(u32[32]{0:T(128)} %constant.161) | copy-start | bytes 388
  373.1 13.5 %copy-start.10 = (bf16[256,1024]{1,0:T(8,128)(2,1)S(1)}, bf16[256,1024]{1,0:T(8,128)(2,1)}, u32[]{:S(2)}) copy-start(bf16[256,1024]{1,0:T(8,128)(2,1)} %param.25) | copy-start | bytes 1572868
  373.1 25.6 %copy-start.20 = (f32[1024]{0:T(1024)S(1)}, f32[1024]{0:T(1024)}, u32[]{:S(2)}) copy-start(f32[1024]{0:T(1024)} %param.34) | copy-start | bytes 12292
  373.1 25.6 %copy-start.26 = (f32[1024]{0:T(1024)S(1)}, f32[1024]{0:T(1024)}, u32[]{:S(2)}) copy-start(f32[1024]{0:T(1024)} %param.33) | copy-start | bytes 12292
  378.5 23.6 %copy-start.41 = (f32[1024]{0:T(1024)S(1)}, f32[1024]{0:T(1024)}, u32[]{:S(2)}) copy-start(f32[1024]{0:T(1024)} %param.40) | copy-start | bytes 12292
  380.4 18.4 %all-to-all-start.1 = ((bf16[4,256,256]{1,2,0:T(8,128)(2,1)}), bf16[4,256,256]{1,2,0:T(8,128)(2,1)}, u32[]{:S(2)}, u32[]{:S(2)}) async-start(bf16[4,256,256]{1,2,0:T(8,128)(2,1)} %copy.115), calls=%async_computation.1 | async-start | bytes 1048576 | tf_op jit(solution)/shard_map/all_to_all | solution.py:166
  398.8 3.3 copy-start.12
  400.8 1.0 copy-start.11
  402.1 6.0 copy-start.23
  402.1 6.0 copy-start.28
  402.1 6.0 copy-start.40
  429.9 6.4 copy-start.34
  430.0 6.3 copy-start.35
  430.0 6.3 copy-start.36
  430.0 6.3 copy-start.37
  430.0 6.3 copy-start.38
  430.0 50.7 %copy-start.18 = (bf16[128,1024]{1,0:T(8,128)(2,1)S(1)}, bf16[128,1024]{1,0:T(8,128)(2,1)}, u32[]{:S(2)}) copy-start(bf16[128,1024]{1,0:T(8,128)(2,1)} %reduce-scatter.7.cloned.1.call-done) | copy-start | bytes 786436
Sparse Core Ops, SparseCore 0:
  173.8 40.3 reduce-scatter.6
  218.0 71.2 reduce-scatter.8
  345.1 59.9 reduce-scatter.4
  408.8 71.7 reduce-scatter.10
where the time goes:
time: 716 us; the launch traced here: 704 us
  blocking collectives  309 us (43%)
  matrix products  172 us (24%)
  waiting for transfers between devices  90.9 us (13%)
  local copies, waits for them, and re-layouts  58.6 us (8%)
  other arithmetic  35.6 us (5%)
  between operations  16 us (2%)
  starting transfers between devices  14.3 us (2%)
  loops' own time  8.54 us (1%)
    psum x1, blocking collectives, body(): lax.psum((ln1_gain_grad, ln1_bias_grad, qkv_weight_grad, query_bias_grad,...  217 us
    all_to_all x1, blocking collectives, body(): lax.all_to_all(stacked, 'head', split_axis=0, concat_axis=2, tiled=True)  52 us
    all_to_all x1, waiting for transfers between devices, forward(): lax.all_to_all(projected, 'head', split_axis=2, concat_axis=0, tiled=True)  48 us
    dot_general x4, matrix products, times_transpose(): lax.dot_general(left, right, (((1,), (1,)), ((), ())), preferred_element_...  26.5 us
    dot_general x2, matrix products, forward(): jnp.dot(active, down_weight, preferred_element_type=jnp.float32) + down_bias  26.3 us
    dot_general x4, matrix products, contract_rows(): lax.dot_general(left, right, (((0,), (0,)), ((), ())), preferred_element_...  23.7 us
    unnamed x1, blocking collectives  23.2 us
    dot_general x6, matrix products, block_scores(): jnp.einsum('qhd,khd->hqk', query_rows, keys, preferred_element_type=jnp.f...  21.8 us
  transfers between devices with their start and end apart: 7, of which 4 were waited for; matrix products, arithmetic and copies ran while one was open for 24% of the time, Pallas kernels for 0%

commit v1 on v0

v1 whole, which is shorter than its diff:
```python
import functools
import math

import jax
import jax.numpy as jnp
from jax import lax
from jax.experimental import pallas as pl
from jax.experimental.pallas import tpu as pltpu
from jax.sharding import PartitionSpec as P

HEAD_DIM = 64
EPSILON = 1e-06
NEGATIVE = -1e30
MIB = 1024 * 1024
F32 = jnp.float32
BF16 = jnp.bfloat16


def dot_nn(left, right):
    return lax.dot_general(left, right, (((1,), (0,)), ((), ())), preferred_element_type=F32)


def dot_nt(left, right):
    return lax.dot_general(left, right, (((1,), (1,)), ((), ())), preferred_element_type=F32)


def dot_tn(left, right):
    return lax.dot_general(left, right, (((0,), (0,)), ((), ())), preferred_element_type=F32)


def unit_norm(values):
    average = jnp.mean(values, -1, keepdims=True)
    centered = values - average
    inverse = lax.rsqrt(jnp.mean(centered * centered, -1, keepdims=True) + EPSILON)
    return centered * inverse, inverse


def norm_back(grad_unit, unit_rows, inverse):
    first_term = jnp.mean(grad_unit, -1, keepdims=True)
    second_term = jnp.mean(grad_unit * unit_rows, -1, keepdims=True)
    return inverse * (grad_unit - first_term - unit_rows * second_term)


def column_sum(values):
    return jnp.sum(values, 0, keepdims=True)


def head_mask(rows, half):
    lane = lax.broadcasted_iota(jnp.int32, (rows, 2 * HEAD_DIM), 1)
    return (lane >= half * HEAD_DIM) & (lane < (half + 1) * HEAD_DIM)


def call(kernel, grid, scalars, in_specs, out_specs, out_shape, scratch, flops, nbytes, vmem=40):
    return pl.pallas_call(
        kernel,
        grid_spec=pltpu.PrefetchScalarGridSpec(
            num_scalar_prefetch=scalars,
            grid=grid,
            in_specs=in_specs,
            out_specs=out_specs,
            scratch_shapes=scratch,
        ),
        out_shape=out_shape,
        compiler_params=pltpu.CompilerParams(vmem_limit_bytes=vmem * MIB),
        cost_estimate=pl.CostEstimate(flops=flops, bytes_accessed=nbytes, transcendentals=0),
    )


def const(shape):
    zeros = (0,) * len(shape)
    return pl.BlockSpec(shape, lambda *_: zeros)


def qkv_kernel(where, tok, gain, bias, wq, wk, wv, bq, bv, qkv, unit):
    rows, _ = unit_norm(tok[...].astype(F32))
    unit[...] = rows.astype(BF16)
    normed = (rows * gain[...] + bias[...]).astype(BF16)
    wide = wq.shape[1]
    qkv[:, :wide] = (dot_nn(normed, wq[...]) + bq[...]).astype(BF16)
    qkv[:, wide : 2 * wide] = dot_nn(normed, wk[...]).astype(BF16)
    qkv[:, 2 * wide :] = (dot_nn(normed, wv[...]) + bv[...]).astype(BF16)


def qkv_forward(order, tokens_all, gain, bias, weight, query_bias, value_bias, heads, rows):
    length, width = tokens_all.shape
    wide = width // heads
    column = lambda part: pl.BlockSpec((width, wide), lambda k, o: (0, part * heads + o[0]))
    return call(
        qkv_kernel,
        (length // rows,),
        1,
        [
            pl.BlockSpec((rows, width), lambda k, o: (k, 0)),
            const((1, width)),
            const((1, width)),
            column(0),
            column(1),
            column(2),
            pl.BlockSpec((1, wide), lambda k, o: (0, o[0])),
            pl.BlockSpec((1, wide), lambda k, o: (0, o[0])),
        ],
        [
            pl.BlockSpec((rows, 3 * wide), lambda k, o: (k, 0)),
            pl.BlockSpec((rows, width), lambda k, o: (k, 0)),
        ],
        [
            jax.ShapeDtypeStruct((length, 3 * wide), BF16),
            jax.ShapeDtypeStruct((length, width), BF16),
        ],
        [],
        6 * length * width * wide,
        length * width * 8,
    )(order, tokens_all, gain, bias, weight, weight, weight, query_bias, value_bias)


def attend_kernel(order, q_ref, k_ref, v_ref, lab_q, lab_k, mixed, lse):
    rows, wide = q_ref.shape
    bias = jnp.where(lab_q[...] == lab_k[...], 0.0, NEGATIVE)
    for pair in range(wide // 128):
        lanes = slice(pair * 128, pair * 128 + 128)
        keys = k_ref[:, lanes]
        values = v_ref[:, lanes]
        queries = q_ref[:, lanes].astype(F32) * (HEAD_DIM**-0.5)
        done = []
        for half in range(2):
            own = jnp.where(head_mask(rows, half), queries, 0.0).astype(BF16)
            scores = dot_nt(own, keys) + bias
            highest = jnp.max(scores, -1, keepdims=True)
            weights = jnp.exp(scores - highest)
            total = jnp.sum(weights, -1, keepdims=True)
            done.append(dot_nn(weights.astype(BF16), values) / total)
            logsum = highest + jnp.log(total)
            spread = jnp.transpose(jnp.broadcast_to(logsum, (rows, 128)))
            lse[0, pl.ds(2 * pair + half, 1), :] = spread[0:1, :]
        mixed[0, :, lanes] = jnp.where(head_mask(rows, 0), done[0], done[1]).astype(BF16)


def attend(order, qkv, lab_col, lab_row, heads, rows):
    length = qkv.shape[0]
    wide = qkv.shape[1] // 3
    return call(
        attend_kernel,
        (heads,),
        1,
        [
            pl.BlockSpec((rows, wide), lambda k, o: (o[k], 0)),
            pl.BlockSpec((length, wide), lambda k, o: (0, 1)),
            pl.BlockSpec((length, wide), lambda k, o: (0, 2)),
            pl.BlockSpec((rows, 1), lambda k, o: (o[k], 0)),
            const((1, length)),
        ],
        [
            pl.BlockSpec((1, rows, wide), lambda k, o: (k, 0, 0)),
            pl.BlockSpec((1, 8, rows), lambda k, o: (k, 0, 0)),
        ],
        [
            jax.ShapeDtypeStruct((heads, rows, wide), BF16),
            jax.ShapeDtypeStruct((heads, 8, rows), F32),
        ],
        [],
        16 * length * length * wide,
        length * wide * 10,
    )(order, qkv, qkv, qkv, lab_col, lab_row)


def project_kernel(heads, order, *refs):
    pieces = refs[:heads]
    tok, out_w, out_b, scale, gain, bias, mixed, attended, middle, normed, total, piece = refs[heads:]
    k = pl.program_id(0)
    for j in range(heads):

        @pl.when(k == j)
        def _():
            piece[...] = pieces[j][...].reshape(piece.shape)

    mixed[...] = piece[...]
    part = dot_nn(piece[...], out_w[...])

    @pl.when(k == 0)
    def _():
        total[...] = part

    @pl.when(k > 0)
    def _():
        total[...] += part

    @pl.when(k == heads - 1)
    def _():
        result = total[...] + out_b[...]
        attended[...] = result
        after = tok[...].astype(F32) + scale[...] * result
        middle[...] = after
        normed[...] = (unit_norm(after)[0] * gain[...] + bias[...]).astype(BF16)


def project(order, mixed_x, received, tokens, out_weight, out_bias, scale, gain, bias):
    heads, rows, wide = mixed_x.shape
    width = tokens.shape[1]
    flat = const((rows, width))
    vector = const((1, width))
    return call(
        functools.partial(project_kernel, heads),
        (heads,),
        1,
        [const((1, rows, wide))]
        + [const((rows, wide))] * (heads - 1)
        + [flat, pl.BlockSpec((wide, width), lambda k, o: (o[k], 0))]
        + [vector] * 4,
        [pl.BlockSpec((rows, wide), lambda k, o: (0, o[k])), flat, flat, flat],
        [
            jax.ShapeDtypeStruct((rows, width), BF16),
            jax.ShapeDtypeStruct((rows, width), F32),
            jax.ShapeDtypeStruct((rows, width), F32),
            jax.ShapeDtypeStruct((rows, width), BF16),
        ],
        [pltpu.VMEM((rows, width), F32), pltpu.VMEM((rows, wide), BF16)],
        2 * rows * width * width,
        width * width * 2 + rows * width * 14,
    )(order, mixed_x, *received, tokens, out_weight, out_bias, scale, gain, bias)


def gelu_parts(values):
    size = jnp.abs(values)
    t = 1.0 / (1.0 + (0.3275911 / math.sqrt(2.0)) * size)
    bell = jnp.exp(-0.5 * values * values)
    poly = 0.5 * 1.061405429
    for term in (-1.453152027, 1.421413741, -0.284496736, 0.254829592):
        poly = poly * t + 0.5 * term
    tail = poly * t * bell
    share = jnp.where(values >= 0, 1.0 - tail, tail)
    slope = share + values * bell * (1.0 / math.sqrt(2.0 * math.pi))
    return values * share, slope


def ffn_kernel(core, n_own, n_other, g_own, g_other, up, up_b, down, down_out, grad_out, up_g, down_g, bias_g, rows_in, rows_t, grads):
    step = pl.program_id(0)
    rows = n_own.shape[0]

    @pl.when(step == 0)
    def _():
        rows_in[:rows] = n_own[...]
        rows_in[rows:] = n_other[...]
        rows_t[:, :rows] = jnp.transpose(n_own[...])
        rows_t[:, rows:] = jnp.transpose(n_other[...])
        grads[:rows] = g_own[...]
        grads[rows:] = g_other[...]

    upward = dot_nn(rows_in[...], up[...]) + up_b[...]
    active, slope = gelu_parts(upward)
    active = active.astype(BF16)
    grad_active = dot_nt(grads[...], down[...])
    grad_up = (grad_active * slope).astype(BF16)
    bias_g[...] = jnp.broadcast_to(column_sum(grad_up.astype(F32)), bias_g.shape)
    downward = dot_nn(active, down[...])
    grad_rows = dot_nt(grad_up, up[...])

    @pl.when(step == 0)
    def _():
        down_out[...] = downward
        grad_out[...] = grad_rows

    @pl.when(step > 0)
    def _():
        down_out[...] += downward
        grad_out[...] += grad_rows

    down_g[...] = dot_tn(active, grads[...]).astype(BF16)
    up_g[...] = dot_nn(rows_t[...], grad_up).astype(BF16)


def ffn(core, n_own, n_other, g_own, g_other, up, up_bias, down, blocks, block):
    rows, width = n_own.shape
    flat = const((rows, width))
    both = const((2 * rows, width))
    return call(
        ffn_kernel,
        (blocks,),
        1,
        [
            flat,
            flat,
            flat,
            flat,
            pl.BlockSpec((width, block), lambda i, c: (0, 2 * i + c[0])),
            pl.BlockSpec((1, block), lambda i, c: (0, 2 * i + c[0])),
            pl.BlockSpec((block, width), lambda i, c: (2 * i + c[0], 0)),
        ],
        [
            both,
            both,
            pl.BlockSpec((width, block), lambda i, c: (0, i)),
            pl.BlockSpec((block, width), lambda i, c: (i, 0)),
            pl.BlockSpec((8, block), lambda i, c: (0, i)),
        ],
        [
            jax.ShapeDtypeStruct((2 * rows, width), F32),
            jax.ShapeDtypeStruct((2 * rows, width), F32),
            jax.ShapeDtypeStruct((width, blocks * block), BF16),
            jax.ShapeDtypeStruct((blocks * block, width), BF16),
            jax.ShapeDtypeStruct((8, blocks * block), F32),
        ],
        [
            pltpu.VMEM((2 * rows, width), BF16),
            pltpu.VMEM((width, 2 * rows), BF16),
            pltpu.VMEM((2 * rows, width), BF16),
        ],
        12 * 2 * rows * width * blocks * block,
        width * blocks * block * 8 + rows * width * 20,
        50,
    )(core, n_own, n_other, g_own, g_other, up, up_bias, down)


def middle_kernel(heads, order, own, other, cot, middle, attended, gain, scale, out_w, grad_mid, grad_att, sums, pieces):
    k = pl.program_id(0)

    @pl.when(k == 0)
    def _():
        grad_rows = own[...] + other[...]
        unit, inverse = unit_norm(middle[...])
        result = cot[...].astype(F32) + norm_back(grad_rows * gain[...], unit, inverse)
        grad_mid[...] = result
        low = (scale[...] * result).astype(BF16)
        grad_att[...] = low
        sums[0:1] = column_sum(grad_rows * unit)
        sums[1:2] = column_sum(grad_rows)
        sums[2:3] = column_sum(result * attended[...])
        sums[3:4] = column_sum(low.astype(F32))
        sums[4:8] = jnp.zeros((4, sums.shape[1]), F32)

    pieces[0] = dot_nt(grad_att[...], out_w[...]).astype(BF16)


def middle_back(order, own, other, cot, middle, attended, gain, scale, out_weight, heads):
    rows, width = cot.shape
    wide = width // heads
    flat = const((rows, width))
    vector = const((1, width))
    return call(
        functools.partial(middle_kernel, heads),
        (heads,),
        1,
        [flat] * 5 + [vector] * 2 + [pl.BlockSpec((wide, width), lambda k, o: (o[k], 0))],
        [flat, flat, const((8, width)), pl.BlockSpec((1, rows, wide), lambda k, o: (k, 0, 0))],
        [
            jax.ShapeDtypeStruct((rows, width), F32),
            jax.ShapeDtypeStruct((rows, width), BF16),
            jax.ShapeDtypeStruct((8, width), F32),
            jax.ShapeDtypeStruct((heads, rows, wide), BF16),
        ],
        [],
        2 * rows * width * width,
        width * width * 2 + rows * width * 24,
    )(order, own, other, cot, middle, attended, gain, scale, out_weight)


def attend_back_kernel(heads, order, *refs):
    pieces = refs[:heads]
    q_ref, k_ref, v_ref, mixed, lse, lab_k, lab_q, grad, sums, grad_k, grad_v, rows_g = refs[heads:]
    step = pl.program_id(0)
    rows, wide = q_ref.shape
    length = k_ref.shape[0]
    chunk = min(256, length)
    for j in range(heads):

        @pl.when(step == j)
        def _():
            rows_g[...] = pieces[j][...].reshape(rows_g.shape)

    @pl.when(step == 0)
    def _():
        grad_k[...] = jnp.zeros_like(grad_k)
        grad_v[...] = jnp.zeros_like(grad_v)

    start = pl.multiple_of(order[step] * rows, rows)
    ones = jnp.ones((8, 128), F32)
    for pair in range(wide // 128):
        lanes = slice(pair * 128, pair * 128 + 128)
        queries = q_ref[:, lanes].astype(F32) * (HEAD_DIM**-0.5)
        grad_rows = rows_g[:, lanes].astype(F32)
        product = grad_rows * mixed[0, :, lanes].astype(F32)
        done = []
        for half in range(2):
            mask = head_mask(rows, half)
            own_q = jnp.where(mask, queries, 0.0).astype(BF16)
            own_g = jnp.where(mask, grad_rows, 0.0).astype(BF16)
            balance = lax.dot_general(
                ones,
                jnp.where(mask, product, 0.0),
                (((1,), (1,)), ((), ())),
                precision=lax.Precision.HIGHEST,
                preferred_element_type=F32,
            )[0:1]
            logsum = lse[0, pl.ds(2 * pair + half, 1), :]
            grad_q = jnp.zeros((rows, 128), F32)
            for part in range(length // chunk):
                here = slice(part * chunk, part * chunk + chunk)
                same = lab_k[here, :] == lab_q[...]
                scores = dot_nt(k_ref[here, lanes], own_q)
                probs = jnp.exp(jnp.where(same, scores - logsum, NEGATIVE))
                grad_probs = dot_nt(v_ref[here, lanes], own_g)
                grad_scores = (probs * (grad_probs - balance)).astype(BF16)
                grad_v[here, lanes] += dot_nn(probs.astype(BF16), own_g)
                grad_k[here, lanes] += dot_nn(grad_scores, own_q)
                grad_q += dot_tn(grad_scores, k_ref[here, lanes])
            done.append(grad_q * (HEAD_DIM**-0.5))
        grad[pl.ds(start, rows), lanes] = jnp.where(head_mask(rows, 0), done[0], done[1]).astype(BF16)

    @pl.when(step == heads - 1)
    def _():
        grad[:, wide : 2 * wide] = grad_k[...].astype(BF16)
        grad[:, 2 * wide :] = grad_v[...].astype(BF16)
        sums[...] = jnp.broadcast_to(column_sum(grad[...].astype(F32)), sums.shape)


def attend_back(order, own_x, received, qkv, mixed_x, lse, lab_col, lab_row):
    heads, rows, wide = mixed_x.shape
    length = qkv.shape[0]
    return call(
        functools.partial(attend_back_kernel, heads),
        (heads,),
        1,
        [const((1, rows, wide))]
        + [const((rows, wide))] * (heads - 1)
        + [
            pl.BlockSpec((rows, wide), lambda k, o: (o[k], 0)),
            pl.BlockSpec((length, wide), lambda k, o: (0, 1)),
            pl.BlockSpec((length, wide), lambda k, o: (0, 2)),
            pl.BlockSpec((1, rows, wide), lambda k, o: (k, 0, 0)),
            pl.BlockSpec((1, 8, rows), lambda k, o: (k, 0, 0)),
            const((length, 1)),
            pl.BlockSpec((1, rows), lambda k, o: (0, o[k])),
        ],
        [const((length, 3 * wide)), const((8, 3 * wide))],
        [
            jax.ShapeDtypeStruct((length, 3 * wide), BF16),
            jax.ShapeDtypeStruct((8, 3 * wide), F32),
        ],
        [
            pltpu.VMEM((length, wide), F32),
            pltpu.VMEM((length, wide), F32),
            pltpu.VMEM((rows, wide), BF16),
        ],
        40 * length * length * wide,
        length * wide * 20,
    )(order, own_x, *received, qkv, qkv, qkv, mixed_x, lse, lab_col, lab_row)


def qkv_grad_kernel(slots, order, unit, grad, wq, wk, wv, gain, bias, sums, small, packed):
    wide = wq.shape[1]
    rows = unit.shape[1]
    product = dot_tn(unit[...], grad[...])
    totals = sums[0:1, :]
    packed[:, : 3 * wide] = (gain[...] * product + bias[...] * totals).astype(BF16)
    gain_g = jnp.zeros((rows, 1), F32)
    bias_g = jnp.zeros((rows, 1), F32)
    for part, weight in enumerate((wq, wk, wv)):
        here = slice(part * wide, part * wide + wide)
        weights = weight[...].astype(F32)
        gain_g += jnp.sum(product[:, here] * weights, -1, keepdims=True)
        bias_g += jnp.sum(totals[:, here] * weights, -1, keepdims=True)
    columns = jnp.transpose(small[...])
    lane = lax.broadcasted_iota(jnp.int32, columns.shape, 1)
    columns = jnp.where(lane == slots, gain_g, jnp.where(lane == slots + 1, bias_g, columns))
    packed[:, 3 * wide :] = columns.astype(BF16)


def qkv_grad(order, unit, grad, weight, gain, bias, sums, small, slots, heads):
    length, width = unit.shape
    wide = width // heads
    rows = 256
    column = lambda part: pl.BlockSpec((rows, wide), lambda k, o: (k, part * heads + o[0]))
    return call(
        functools.partial(qkv_grad_kernel, slots),
        (width // rows,),
        1,
        [
            pl.BlockSpec((length, rows), lambda k, o: (0, k)),
            const((length, 3 * wide)),
            column(0),
            column(1),
            column(2),
            pl.BlockSpec((rows, 1), lambda k, o: (k, 0)),
            pl.BlockSpec((rows, 1), lambda k, o: (k, 0)),
            const((8, 3 * wide)),
            pl.BlockSpec((128, rows), lambda k, o: (0, k)),
        ],
        [pl.BlockSpec((rows, 3 * wide + 128), lambda k, o: (k, 0))],
        [jax.ShapeDtypeStruct((width, 3 * wide + 128), BF16)],
        [],
        6 * length * width * wide,
        length * width * 2 + length * wide * 6 + width * wide * 14,
    )(order, unit, grad, weight, weight, weight, gain, bias, sums, small)[0]


def input_kernel(heads, order, *refs):
    pieces = refs[:heads]
    wq, wk, wv, tok, gain, grad_mid, out, total, piece = refs[heads:]
    k = pl.program_id(0)
    wide = wq.shape[1]
    for j in range(heads):

        @pl.when(k == j)
        def _():
            piece[...] = pieces[j][...]

    part = dot_nt(piece[:, :wide], wq[...])
    part += dot_nt(piece[:, wide : 2 * wide], wk[...])
    part += dot_nt(piece[:, 2 * wide :], wv[...])

    @pl.when(k == 0)
    def _():
        total[...] = part

    @pl.when(k > 0)
    def _():
        total[...] += part

    @pl.when(k == heads - 1)
    def _():
        unit, inverse = unit_norm(tok[...].astype(F32))
        out[...] = grad_mid[...] + norm_back(total[...] * gain[...], unit, inverse)


def input_back(order, grad, received, weight, tokens, gain, grad_mid, heads):
    rows, width = tokens.shape
    wide = width // heads
    flat = const((rows, width))
    column = lambda part: pl.BlockSpec((width, wide), lambda k, o: (0, part * heads + o[k]))
    return call(
        functools.partial(input_kernel, heads),
        (heads,),
        1,
        [pl.BlockSpec((rows, 3 * wide), lambda k, o: (o[0], 0))]
        + [const((rows, 3 * wide))] * (heads - 1)
        + [column(0), column(1), column(2), flat, const((1, width)), flat],
        [flat],
        [jax.ShapeDtypeStruct((rows, width), F32)],
        [pltpu.VMEM((rows, width), F32), pltpu.VMEM((rows, 3 * wide), BF16)],
        6 * rows * width * width,
        width * width * 6 + rows * width * 16,
    )(order, grad, *received, weight, weight, weight, tokens, gain, grad_mid)[0]


def exchange(value, axis, distance):
    size = lax.axis_size(axis)
    return lax.ppermute(value, axis, [(i, i ^ distance) for i in range(size)])


def pick(stacked, index):
    return lax.dynamic_index_in_dim(stacked, index, 0, keepdims=False)


def body(
    tokens,
    cotangent,
    image_counts,
    ln1_gain,
    ln1_bias,
    qkv_weight,
    query_bias,
    value_bias,
    out_weight,
    out_bias,
    scale_attn,
    ln2_gain,
    ln2_bias,
    up_weight,
    up_bias,
    down_weight,
    down_bias,
    scale_mlp,
):
    rows, width = tokens.shape
    hidden = up_weight.shape[1]
    heads = lax.axis_size("head")
    seqs = lax.axis_size("seq")
    places = seqs // 2
    me = lax.axis_index("head")
    seq = lax.axis_index("seq")
    core = seq % 2
    place = seq // 2
    length = rows * heads
    wide = width // heads
    block = hidden // seqs
    share = width // seqs
    order = (me ^ jnp.arange(heads, dtype=jnp.int32)).astype(jnp.int32)
    groups = [[2 * i + c for i in range(places)] for c in range(2)]

    boundary = jnp.cumsum(image_counts[0])
    spots = jnp.arange(length, dtype=jnp.int32)
    labels = jnp.sum((spots[:, None] >= boundary[None, :]).astype(jnp.int32), 1)
    lab_col = labels.reshape(length, 1)
    lab_row = labels.reshape(1, length)
    line = lambda vector: vector.reshape(1, -1)

    tokens_all = lax.all_gather(tokens, "head", axis=0, tiled=True)
    grad_output = cotangent.astype(F32)
    grad_down = (scale_mlp * grad_output).astype(BF16)
    down_bias_grad = jnp.sum(grad_down.astype(F32), 0)
    grad_down_other = exchange(grad_down, "seq", 1)

    qkv, unit1 = qkv_forward(
        order,
        tokens_all,
        line(ln1_gain),
        line(ln1_bias),
        qkv_weight,
        line(query_bias),
        line(value_bias),
        heads,
        rows,
    )
    mixed_x, lse = attend(order, qkv, lab_col, lab_row, heads, rows)
    received = [exchange(mixed_x[k], "head", k) for k in range(1, heads)]
    mixed, attended, middle, normed2 = project(
        order,
        mixed_x,
        received,
        tokens,
        out_weight,
        line(out_bias),
        line(scale_attn),
        line(ln2_gain),
        line(ln2_bias),
    )
    normed2_other = exchange(normed2, "seq", 1)
    core_index = core.astype(jnp.int32).reshape(1)
    down_sum, grad_sum, up_g, down_g, up_bias_g = ffn(
        core_index,
        normed2,
        normed2_other,
        grad_down,
        grad_down_other,
        up_weight,
        line(up_bias),
        down_weight,
        places,
        block,
    )
    grad_other = exchange(grad_sum[rows:], "seq", 1)
    down_other = exchange(down_sum[rows:], "seq", 1)
    grad_middle, grad_attended, sums2, grad_x = middle_back(
        order,
        grad_sum,
        grad_other,
        cotangent,
        middle,
        attended,
        line(ln2_gain),
        line(scale_attn),
        out_weight,
        heads,
    )
    grad_received = [exchange(grad_x[k], "head", k) for k in range(1, heads)]

    downward = down_sum[:rows] + down_other + down_bias
    output = (middle + scale_mlp * downward).astype(BF16)
    scale_mlp_grad = jnp.sum(grad_output * downward, 0)

    down_part = lax.psum_scatter(down_g, "seq", scatter_dimension=0, axis_index_groups=groups, tiled=True)
    up_part = lax.psum_scatter(up_g, "seq", scatter_dimension=0, axis_index_groups=groups, tiled=True)

    split = mixed.reshape(rows, places, 2, share)
    mine = lax.dynamic_index_in_dim(split, core, 2, keepdims=False).reshape(rows, width // 2)
    theirs = lax.dynamic_index_in_dim(split, 1 - core, 2, keepdims=False).reshape(rows, width // 2)
    mixed_other = exchange(theirs, "seq", 1)
    attended_other = exchange(grad_attended, "seq", 1)
    out_g = (dot_tn(mine, grad_attended) + dot_tn(mixed_other, attended_other)).astype(BF16)
    out_blocks = out_g.reshape(places, share, width)
    out_part = pick(out_blocks, place).astype(F32)
    for j in range(1, places):
        out_part += exchange(pick(out_blocks, place ^ j), "seq", 2 * j).astype(F32)

    grad_qkv, qkv_sums = attend_back(order, grad_x, grad_received, qkv, mixed_x, lse, lab_col, lab_row)
    pieces = grad_qkv.reshape(heads, rows, 3 * wide)
    back = [exchange(pick(pieces, order[k]), "head", k) for k in range(1, heads)]
    tokens_grad = input_back(order, grad_qkv, back, qkv_weight, tokens, line(ln1_gain), grad_middle, heads)

    nothing = jnp.zeros((width,), F32)
    query_g = lax.dynamic_update_slice(nothing, qkv_sums[0, :wide], (me * wide,))
    value_g = lax.dynamic_update_slice(nothing, qkv_sums[0, 2 * wide :], (me * wide,))
    many = hidden // width
    spread = jnp.zeros((places, 2, block), F32)
    spread = lax.dynamic_update_slice(spread, up_bias_g[0].reshape(places, 1, block), (0, core, 0))
    spread = spread.reshape(seqs, many, share).transpose(1, 0, 2).reshape(many, width)
    vectors = [
        query_g,
        value_g,
        sums2[0],
        sums2[1],
        sums2[2],
        sums2[3],
        down_bias_grad,
        scale_mlp_grad,
    ]
    slots = len(vectors) + many
    small = jnp.concatenate(
        [jnp.stack(vectors), spread, jnp.zeros((128 - slots, width), F32)], 0
    )
    packed = qkv_grad(
        order,
        unit1,
        grad_qkv,
        qkv_weight,
        ln1_gain.reshape(width, 1),
        ln1_bias.reshape(width, 1),
        qkv_sums,
        small,
        slots,
        heads,
    )
    wider = 3 * wide + 128
    by_core = packed.reshape(places, 2, share, wider)
    keep = lax.dynamic_index_in_dim(by_core, core, 1, keepdims=False)
    give = lax.dynamic_index_in_dim(by_core, 1 - core, 1, keepdims=False)
    chip = (keep.astype(F32) + exchange(give, "seq", 1).astype(F32)).astype(BF16)
    total = pick(chip, place).astype(F32)
    for j in range(1, places):
        total += exchange(pick(chip, place ^ j), "seq", 2 * j).astype(F32)
    total = total.astype(BF16)
    gathered = [total] + [exchange(total, "head", k) for k in range(1, heads)]
    ordered = []
    for j in range(heads):
        choice = gathered[0]
        for k in range(1, heads):
            choice = jnp.where((me ^ k) == j, gathered[k], choice)
        ordered.append(choice)
    qkv_weight_grad = jnp.stack([item[:, : 3 * wide].reshape(share, 3, wide) for item in ordered], 2)
    qkv_weight_grad = qkv_weight_grad.reshape(share, 3 * width).astype(F32)
    columns = sum(item[:, 3 * wide :].astype(F32) for item in gathered)
    small_out = columns[:, : slots + 2].T

    up_part = up_part.reshape(-1, width)
    rest = jnp.concatenate([down_part, up_part, out_part.astype(BF16)], 0)
    rest = lax.psum(rest, "head").astype(F32)
    cut = down_part.shape[0]
    edge = cut + up_part.shape[0]
    down_weight_grad = rest[:cut]
    out_weight_grad = rest[edge:]
    up_half = rest[cut:edge].astype(BF16).reshape(2, share, places * block)
    up_mine = pick(up_half, core)
    up_theirs = exchange(pick(up_half, 1 - core), "seq", 1)
    first = jnp.where(core == 0, up_mine, up_theirs).reshape(share, places, 1, block)
    second = jnp.where(core == 0, up_theirs, up_mine).reshape(share, places, 1, block)
    up_weight_grad = jnp.concatenate([first, second], 2).reshape(share, hidden).astype(F32)

    up_bias_grad = small_out[8 : 8 + many].reshape(hidden // seqs)
    return (
        output,
        tokens_grad,
        small_out[slots],
        small_out[slots + 1],
        qkv_weight_grad,
        small_out[0],
        small_out[1],
        out_weight_grad,
        small_out[5],
        small_out[4],
        small_out[2],
        small_out[3],
        up_weight_grad,
        up_bias_grad,
        down_weight_grad,
        small_out[6],
        small_out[7],
    )


def solution(mesh):
    rows = P(("seq", "head"), None)
    flat = P("seq")
    tall = P("seq", None)
    in_specs = (rows, rows, tall) + (P(),) * 15
    out_specs = (
        rows,
        rows,
        flat,
        flat,
        tall,
        flat,
        flat,
        tall,
        flat,
        flat,
        flat,
        flat,
        tall,
        flat,
        tall,
        flat,
        flat,
    )
    return jax.shard_map(body, mesh=mesh, in_specs=in_specs, out_specs=out_specs, check_vma=False)
```

time: 716 us -> 410 us (0.57); the launches traced: 704 us -> 409 us
  blocking collectives: 309 us -> 0 us
  matrix products: 172 us -> 3.24 us
  waiting for transfers between devices: 90.9 us -> 198 us
  Pallas kernels: 0 us -> 78 us
  other arithmetic: 35.6 us -> 19 us
  starting transfers between devices: 14.3 us -> 25.1 us
  loops' own time: 8.54 us -> 0 us
    psum x1 -> x0, blocking collectives: 217 us -> none  [body(): lax.psum((ln1_gain_grad, ln1_bias_grad, qkv_weight_grad, query_bias_grad,...]
    dot_general x32 -> x2, matrix products: 172 us -> 3.24 us  [dot_tn(): lax.dot_general(left, right, (((0,), (0,)), ((), ())), preferred_element_...]
    ppermute x0 -> x26, waiting for transfers between devices: none -> 108 us  [exchange(): return lax.ppermute(value, axis, [(i, i ^ distance) for i in range(size)])]
    pallas_call x0 -> x8, Pallas kernels: none -> 78 us  [the longest x1 22.1 us: ffn(): call(ffn_kernel, (blocks,), 1, [flat, flat, flat, flat, pl.BlockSpec((wid...]
    all_to_all x3 -> x0, waiting for transfers between devices: 73.4 us -> none  [the longest x1 48 us: forward(): lax.all_to_all(projected, 'head', split_axis=2, concat_axis=0, tiled=True)]
    all_to_all x2 -> x0, blocking collectives: 68.6 us -> none  [the longest x1 52 us: body(): lax.all_to_all(stacked, 'head', split_axis=0, concat_axis=2, tiled=True)]
    all_gather x0 -> x1, waiting for transfers between devices: none -> 49.1 us  [body(): tokens_all = lax.all_gather(tokens, 'head', axis=0, tiled=True)]
    unnamed x73 -> x96, local copies, waits for them, and re-layouts: 2.67 us -> 28.8 us
  transfers between devices with their start and end apart: 7 -> 30, of which waited for: 4 -> 16; matrix products, arithmetic and copies ran while one was open for 24% -> 15% of each run, Pallas kernels for 0% -> 10%
where the time goes in v1:
time: 410 us; the launch traced here: 409 us
  waiting for transfers between devices  198 us (48%)
  Pallas kernels  78 us (19%)
  local copies, waits for them, and re-layouts  65.5 us (16%)
  starting transfers between devices  25.1 us (6%)
  between operations  20.2 us (5%)
  other arithmetic  19 us (5%)
    ppermute x26, waiting for transfers between devices, exchange(): return lax.ppermute(value, axis, [(i, i ^ distance) for i in range(size)])  108 us
    all_gather x1, waiting for transfers between devices, body(): tokens_all = lax.all_gather(tokens, 'head', axis=0, tiled=True)  49.1 us
    unnamed x96, local copies, waits for them, and re-layouts  28.8 us
    ppermute x26, starting transfers between devices, exchange(): return lax.ppermute(value, axis, [(i, i ^ distance) for i in range(size)])  24.7 us
    reduce_scatter x1, waiting for transfers between devices, body(): lax.psum_scatter(down_g, 'seq', scatter_dimension=0, axis_index_groups=gr...  23.7 us
    pallas_call x1, Pallas kernels, ffn(): call(ffn_kernel, (blocks,), 1, [flat, flat, flat, flat, pl.BlockSpec((wid...  22.1 us
    pallas_call x1, Pallas kernels, attend_back(): call(functools.partial(attend_back_kernel, heads), (heads,), 1, [const((1...  21.8 us
    psum x1, waiting for transfers between devices, body(): rest = lax.psum(rest, 'head').astype(F32)  15.3 us
  transfers between devices with their start and end apart: 30, of which 16 were waited for; matrix products, arithmetic and copies ran while one was open for 15% of the time, Pallas kernels for 10%

profile of v1, /device:TPU:0, one launch (start us, length us, event | category | flops | bytes accessed | tf_op | source)
XLA Modules:
  0.0 409.0 jit_solution(7216627230039606984)
XLA Ops:
  9.1 49.1 %all-gather.2.cloned.1.call-done.tok = bf16[1024,1024]{1,0:T(8,128)(2,1)} async-done(((bf16[256,1024]{1,0:T(8,128)(2,1)}), bf16[1024,1024]{1,0:T(8,128)(2,1)}) %all-gather.2.cloned.1.call-update) | async-done | bytes 2097168 | tf_op jit(solution)/shard_map/all_gather | solution.py:596
  58.3 2.8 copy-done
  61.1 1.6 copy-done.13
  65.4 4.2 %shard_map.305 = (bf16[1024,768]{1,0:T(8,128)(2,1)S(1)}, bf16[1024,1024]{1,0:T(8,128)(2,1)S(1)}) custom-call(s32[4]{0:T(128)S(1)} %iota_xor_fusion.where.order, bf16[1024,1024]{1,0:T(8,128)(2,1)S(1)} %copy-done.13, f32[1,1024]{1,0:T(1,128)S(1)} %bitcast.111, f32[1,1024]{1,0:T(1,128)S(1)} %bitcast.121, bf16[1024,3072]{1,0:T(8,128)(2,1)S(1)} %copy-done, ...), custom_call_target="tpu_custom_call" | custom-call | flops 1610612736 | bytes 8388608 | tf_op jit(solution)/shard_map/pallas_call | solution.py:88
  69.7 9.9 %shard_map.306 = (bf16[4,256,256]{2,1,0:T(8,128)(2,1)S(1)}, f32[4,8,256]{2,1,0:T(8,128)S(1)}) custom-call(s32[4]{0:T(128)S(1)} %iota_xor_fusion.where.order, bf16[1024,768]{1,0:T(8,128)(2,1)S(1)} %get-tuple-element.36.q_ref.k_ref.v_ref.refs_4_.refs_5_.refs_6_, bf16[1024,768]{1,0:T(8,128)(2,1)S(1)} %get-tuple-element.36.q_ref.k_ref.v_ref.refs_4_.refs_5_.refs_6_, ...), custom_call_target="tpu_custom_call" | custom-call | flops 4294967296 | bytes 2621440 | tf_op jit(solution)/shard_map/pallas_call | solution.py:141
  79.8 1.7 collective-permute-start.1
  81.5 2.7 collective-permute-start.2
  85.1 1.9 collective-permute-done.refs_1_
  87.0 5.7 %collective-permute-done.1.refs_2_ = bf16[256,256]{1,0:T(8,128)(2,1)S(1)} collective-permute-done((bf16[256,256]{1,0:T(8,128)(2,1)S(1)}, bf16[256,256]{1,0:T(8,128)(2,1)S(1)}, u32[]{:S(2)}, u32[]{:S(2)}) %collective-permute-start.1) | collective-permute-done | bytes 131104 | tf_op jit(solution)/shard_map/ppermute | solution.py:546
  92.8 3.6 shard_map.307
  99.2 2.2 collective-permute-done.3.n_other
  101.4 22.1 %shard_map.308 = (f32[512,1024]{1,0:T(8,128)}, f32[512,1024]{1,0:T(8,128)}, bf16[1024,2048]{1,0:T(8,128)(2,1)}, bf16[2048,1024]{1,0:T(8,128)(2,1)}, f32[8,2048]{1,0:T(8,128)S(1)}) custom-call(s32[1]{0:T(128)} %bitcast.15.core, bf16[256,1024]{1,0:T(8,128)(2,1)} %get-tuple-element.39.n_own, bf16[256,1024]{1,0:T(8,128)(2,1)} %collective-permute-done.3.n_other, ...), custom_call_target="tpu_custom_call" | custom-call | flops 12884901888 | bytes 22020096 | tf_op jit(solution)/shard_map/pallas_call | solution.py:275
  124.5 2.4 slice.127
  130.6 2.2 reshape.185
  132.9 3.3 constant_dynamic-slice_fusion.3
  136.1 1.9 copy.92
  138.3 1.9 copy.91
  140.3 1.6 copy-done.4
  141.9 1.3 copy-done.8
  143.2 1.2 copy-done.19
  144.4 5.1 %shard_map.309 = (f32[256,1024]{1,0:T(8,128)S(1)}, bf16[256,1024]{1,0:T(8,128)(2,1)}, f32[8,1024]{1,0:T(8,128)S(1)}, bf16[4,256,256]{2,1,0:T(8,128)(2,1)S(1)}) custom-call(s32[4]{0:T(128)S(1)} %iota_xor_fusion.where.order, f32[512,1024]{1,0:T(8,128)S(1)} %copy-done.4, f32[256,1024]{1,0:T(8,128)} %collective-permute-done.6.other, ...), custom_call_target="tpu_custom_call" | custom-call | flops 536870912 | bytes 8388608 | tf_op jit(solution)/shard_map/pallas_call | solution.py:338
  149.5 2.2 collective-permute-start.7
  152.5 1.6 collective-permute-start.9
  154.3 2.6 fusion.2
  157.3 7.3 %collective-permute-done.8.refs_2_ = bf16[256,256]{1,0:T(8,128)(2,1)S(1)} collective-permute-done((bf16[256,256]{1,0:T(8,128)(2,1)S(1)}, bf16[256,256]{1,0:T(8,128)(2,1)S(1)}, u32[]{:S(2)}, u32[]{:S(2)}) %collective-permute-start.8) | collective-permute-done | bytes 131104 | tf_op jit(solution)/shard_map/ppermute | solution.py:546
  164.7 21.8 %shard_map.310 = (bf16[1024,768]{1,0:T(8,128)(2,1)S(1)}, f32[8,768]{1,0:T(8,128)S(1)}) custom-call(s32[4]{0:T(128)S(1)} %iota_xor_fusion.where.order, bf16[4,256,256]{2,1,0:T(8,128)(2,1)S(1)} %get-tuple-element.43.refs_0_, bf16[256,256]{1,0:T(8,128)(2,1)S(1)} %collective-permute-done.7.refs_1_, bf16[256,256]{1,0:T(8,128)(2,1)S(1)} %collective-permute-done.8.refs_2_, ...), custom_call_target="tpu_custom_call" | custom-call | flops 10737418240 | bytes 5242880 | tf_op jit(solution)/shard_map/pallas_call | solution.py:418
  187.0 1.6 fusion.11
  188.7 1.7 add_convert_fusion
  191.3 2.4 collective-permute-start.24
  194.8 3.0 copy-done.1
  197.8 4.3 %shard_map.312 = bf16[1024,896]{1,0:T(8,128)(2,1)S(1)} custom-call(s32[4]{0:T(128)S(1)} %iota_xor_fusion.where.order, bf16[1024,1024]{1,0:T(8,128)(2,1)S(1)} %copy-done.10, bf16[1024,768]{1,0:T(8,128)(2,1)S(1)} %get-tuple-element.45.refs_0_.grad, bf16[1024,3072]{1,0:T(8,128)(2,1)S(1)} %copy-done.1, bf16[1024,3072]{1,0:T(8,128)(2,1)S(1)} %copy-done.1, ...), custom_call_target="tpu_custom_call" | custom-call | flops 1610612736 | bytes 7340032 | tf_op jit(solution)/shard_map/pallas_call | solution.py:472
  203.2 1.3 copy.79
  204.5 2.7 collective-permute-done.24
  207.2 5.0 %collective-permute-done.23 = bf16[128,1024]{1,0:T(8,128)(2,1)} collective-permute-done((bf16[128,1024]{1,0:T(8,128)(2,1)}, bf16[128,1024]{1,0:T(8,128)(2,1)}, u32[]{:S(2)}, u32[]{:S(2)}) %collective-permute-start.23) | collective-permute-done | bytes 262176 | tf_op jit(solution)/shard_map/ppermute | solution.py:546
  212.1 5.3 %collective-permute-done.22 = bf16[128,1024]{1,0:T(8,128)(2,1)} collective-permute-done((bf16[128,1024]{1,0:T(8,128)(2,1)S(1)}, bf16[128,1024]{1,0:T(8,128)(2,1)}, u32[]{:S(2)}, u32[]{:S(2)}) %collective-permute-start.22) | collective-permute-done | bytes 262176 | tf_op jit(solution)/shard_map/ppermute | solution.py:546
  217.5 1.4 fusion.5
  218.9 1.4 reshape.184
  220.3 23.7 %reduce-scatter.3.cloned.1.call-done = bf16[512,1024]{1,0:T(8,128)(2,1)} async-done(((bf16[2048,1024]{1,0:T(8,128)(2,1)}), bf16[512,1024]{1,0:T(8,128)(2,1)}) %reduce-scatter.3.cloned.1.call-update) | async-done | bytes 1048592 | tf_op jit(solution)/shard_map/reduce_scatter | solution.py:660
  244.0 2.9 pad_maximum_fusion
  246.9 1.2 copy-done.37
  248.1 1.3 copy.90
  249.3 1.7 fusion
  252.8 1.5 collective-permute-start.16
  260.7 1.4 collective-permute-start.15
  263.8 1.5 collective-permute-start.10
  265.3 2.4 collective-permute-start.11
  269.2 1.9 fusion.8
  271.0 3.3 collective-permute-start.19
  274.3 27.0 %collective-permute-done.10.refs_1_ = bf16[256,768]{1,0:T(8,128)(2,1)S(1)} collective-permute-done((bf16[256,768]{1,0:T(8,128)(2,1)S(1)}, bf16[256,768]{1,0:T(8,128)(2,1)S(1)}, u32[]{:S(2)}, u32[]{:S(2)}) %collective-permute-start.10) | collective-permute-done | bytes 393248 | tf_op jit(solution)/shard_map/ppermute | solution.py:546
  301.3 7.3 %collective-permute-done.11.refs_2_ = bf16[256,768]{1,0:T(8,128)(2,1)} collective-permute-done((bf16[256,768]{1,0:T(8,128)(2,1)}, bf16[256,768]{1,0:T(8,128)(2,1)}, u32[]{:S(2)}, u32[]{:S(2)}) %collective-permute-start.11) | collective-permute-done | bytes 393248 | tf_op jit(solution)/shard_map/ppermute | solution.py:546
  308.7 11.2 %collective-permute-done.12.refs_3_ = bf16[256,768]{1,0:T(8,128)(2,1)} collective-permute-done((bf16[256,768]{1,0:T(8,128)(2,1)}, bf16[256,768]{1,0:T(8,128)(2,1)}, u32[]{:S(2)}, u32[]{:S(2)}) %collective-permute-start.12) | collective-permute-done | bytes 393248 | tf_op jit(solution)/shard_map/ppermute | solution.py:546
  319.8 2.8 copy-done.2
  322.6 7.0 %shard_map.311 = f32[256,1024]{1,0:T(8,128)} custom-call(s32[4]{0:T(128)S(1)} %iota_xor_fusion.where.order, bf16[1024,768]{1,0:T(8,128)(2,1)S(1)} %get-tuple-element.45.refs_0_.grad, bf16[256,768]{1,0:T(8,128)(2,1)S(1)} %collective-permute-done.10.refs_1_, bf16[256,768]{1,0:T(8,128)(2,1)} %collective-permute-done.11.refs_2_, ...), custom_call_target="tpu_custom_call" | custom-call | flops 1610612736 | bytes 10485760 | tf_op jit(solution)/shard_map/pallas_call | solution.py:529
  330.3 31.3 %collective-permute-done.18 = bf16[128,896]{0,1:T(8,128)(2,1)} collective-permute-done((bf16[128,896]{0,1:T(8,128)(2,1)}, bf16[128,896]{0,1:T(8,128)(2,1)}, u32[]{:S(2)}, u32[]{:S(2)}) %collective-permute-start.18) | collective-permute-done | bytes 229408 | tf_op jit(solution)/shard_map/ppermute | solution.py:546
  361.7 1.3 select_select_fusion.1
  364.7 1.3 select_select_fusion.3
  370.3 15.3 %all-reduce.2.cloned.1.call-done = bf16[1152,1024]{1,0:T(8,128)(2,1)} async-done(((bf16[1152,1024]{1,0:T(8,128)(2,1)}), bf16[1152,1024]{1,0:T(8,128)(2,1)}) %all-reduce.2.cloned.1.call-update) | async-done | bytes 2359312 | tf_op jit(solution)/shard_map/psum | solution.py:735
  385.6 1.2 slice-done
  388.4 2.9 maximum_convert_fusion.1
  391.3 2.0 reshape.195
  394.7 1.8 slice.189
  396.5 2.8 slice.196
  399.3 1.1 bitcast_select_fusion.1
  400.7 1.8 copy.89
  (168 shorter events, 34.3 us)
Async XLA Ops:
  7.2 51.1 %all-gather.2.cloned.1.call-start = ((), (), s32[]{:S(2)}) async-start(), calls=%async_computation.2 | async-start | bytes 2621440 | tf_op jit(solution)/shard_map/all_gather | solution.py:596
  7.9 211.0 %reduce-scatter.5.cloned.1.call-start = ((), (), s32[]{:S(2)}) async-start(), calls=%async_computation.4 | async-start | bytes 5242880 | tf_op jit(solution)/shard_map/reduce_scatter | solution.py:661
  9.1 60.5 %copy-start.20 = (s32[1024,1]{1,0:T(8,128)}, s32[1024,1]{1,0:T(8,128)S(1)}, u32[]{:S(2)}) copy-start(s32[1024,1]{1,0:T(8,128)S(1)} %copy.73.lab_q.refs_9_) | copy-start | bytes 12292
  58.3 2.8 copy-start
  61.0 1.6 copy-start.13
  69.6 10.0 %copy-start.9 = (bf16[1024,1024]{1,0:T(8,128)(2,1)}, bf16[1024,1024]{1,0:T(8,128)(2,1)S(1)}, u32[]{:S(2)}) copy-start(bf16[1024,1024]{1,0:T(8,128)(2,1)S(1)} %get-tuple-element.47.unit) | copy-start | bytes 6291460
  69.6 10.0 %copy-start.33 = (bf16[1024,768]{1,0:T(8,128)(2,1)}, bf16[1024,768]{1,0:T(8,128)(2,1)S(1)}, u32[]{:S(2)}) copy-start(bf16[1024,768]{1,0:T(8,128)(2,1)S(1)} %get-tuple-element.36.q_ref.k_ref.v_ref.refs_4_.refs_5_.refs_6_) | copy-start | bytes 4718596
  69.6 14.5 %copy-start.5 = (bf16[256,1024]{1,0:T(8,128)(2,1)S(1)}, bf16[256,1024]{1,0:T(8,128)(2,1)}, u32[]{:S(2)}) copy-start(bf16[256,1024]{1,0:T(8,128)(2,1)} %cot.1) | copy-start | bytes 1572868
  69.7 14.5 %copy-start.44 = (f32[1024]{0:T(1024)S(1)}, f32[1024]{0:T(1024)}, u32[]{:S(2)}) copy-start(f32[1024]{0:T(1024)} %param.35) | copy-start | bytes 12292
  69.7 23.1 %copy-start.3 = (bf16[1024,1024]{1,0:T(8,128)(2,1)S(1)}, bf16[1024,1024]{1,0:T(8,128)(2,1)}, u32[]{:S(2)}) copy-start(bf16[1024,1024]{1,0:T(8,128)(2,1)} %out_w.1) | copy-start | bytes 6291460
  69.7 23.1 %copy-start.25 = (f32[1024]{0:T(1024)S(1)}, f32[1024]{0:T(1024)}, u32[]{:S(2)}) copy-start(f32[1024]{0:T(1024)} %param.28) | copy-start | bytes 12292
  69.7 23.1 %copy-start.26 = (f32[1024]{0:T(1024)S(1)}, f32[1024]{0:T(1024)}, u32[]{:S(2)}) copy-start(f32[1024]{0:T(1024)} %param.29) | copy-start | bytes 12292
  69.7 23.1 %copy-start.29 = (f32[1024]{0:T(1024)S(1)}, f32[1024]{0:T(1024)}, u32[]{:S(2)}) copy-start(f32[1024]{0:T(1024)} %param.27) | copy-start | bytes 12292
  69.7 23.1 %copy-start.30 = (f32[1024]{0:T(1024)S(1)}, f32[1024]{0:T(1024)}, u32[]{:S(2)}) copy-start(f32[1024]{0:T(1024)} %param.30) | copy-start | bytes 12292
  79.6 16.8 %copy-start.14 = (bf16[4,256,256]{2,1,0:T(8,128)(2,1)}, bf16[4,256,256]{2,1,0:T(8,128)(2,1)S(1)}, u32[]{:S(2)}) copy-start(bf16[4,256,256]{2,1,0:T(8,128)(2,1)S(1)} %get-tuple-element.37.refs_0_.refs_7_) | copy-start | bytes 1572868
  79.6 13.1 %copy-start.6 = (bf16[256,1024]{1,0:T(8,128)(2,1)S(1)}, bf16[256,1024]{1,0:T(8,128)(2,1)}, u32[]{:S(2)}) copy-start(bf16[256,1024]{1,0:T(8,128)(2,1)} %refs_7_.1) | copy-start | bytes 1572868
  79.7 7.3 %collective-permute-start = (bf16[256,256]{1,0:T(8,128)(2,1)S(1)}, bf16[256,256]{1,0:T(8,128)(2,1)S(1)}, u32[]{:S(2)}, u32[]{:S(2)}) collective-permute-start(bf16[256,256]{1,0:T(8,128)(2,1)S(1)} %get-tuple-element.119), channel_id=1, source_target_pairs={{0,1},{1,0},{2,3},{3,2},{4,5},{5,4},{6,7},{7,6},{8,9},{9,8},{10,11... | collective-permute-start | bytes 393224 | tf_op jit(solution)/shard_map/ppermute | solution.py:546
  79.8 13.0 %collective-permute-start.1 = (bf16[256,256]{1,0:T(8,128)(2,1)S(1)}, bf16[256,256]{1,0:T(8,128)(2,1)S(1)}, u32[]{:S(2)}, u32[]{:S(2)}) collective-permute-start(bf16[256,256]{1,0:T(8,128)(2,1)S(1)} %get-tuple-element.118), channel_id=1, source_target_pairs={{0,2},{1,3},{2,0},{3,1},{4,6},{5,7},{6,4},{7,5},{8,10},{9,11},{10,... | collective-permute-start | bytes 393224 | tf_op jit(solution)/shard_map/ppermute | solution.py:546
  81.5 20.0 %copy-start.35 = (f32[4096]{0:T(1024)S(1)}, f32[4096]{0:T(1024)}, u32[]{:S(2)}) copy-start(f32[4096]{0:T(1024)} %param.32) | copy-start | bytes 49156
  81.5 11.3 %collective-permute-start.2 = (bf16[256,256]{1,0:T(8,128)(2,1)S(1)}, bf16[256,256]{1,0:T(8,128)(2,1)S(1)}, u32[]{:S(2)}, u32[]{:S(2)}) collective-permute-start(bf16[256,256]{1,0:T(8,128)(2,1)S(1)} %get-tuple-element.117), channel_id=1, source_target_pairs={{0,3},{1,2},{2,1},{3,0},{4,7},{5,6},{6,5},{7,4},{8,11},{9,10},{10,... | collective-permute-start | bytes 393224 | tf_op jit(solution)/shard_map/ppermute | solution.py:546
  85.1 14.1 %collective-permute-start.4 = (bf16[256,1024]{1,0:T(8,128)(2,1)}, bf16[256,1024]{1,0:T(8,128)(2,1)}, u32[]{:S(2)}, u32[]{:S(2)}) collective-permute-start(bf16[256,1024]{1,0:T(8,128)(2,1)} %get-tuple-element.90.g_own), channel_id=1, source_target_pairs={{0,4},{4,0},{8,12},{12,8},{16,20},{20,16},{24,28},{28,24},{1,5},{5... | collective-permute-start | bytes 1572872 | tf_op jit(solution)/shard_map/ppermute | solution.py:546
  99.2 2.3 collective-permute-start.3
  123.5 120.5 %reduce-scatter.3.cloned.1.call-start = ((), (), s32[]{:S(2)}) async-start(), calls=%async_computation.3 | async-start | bytes 5242880 | tf_op jit(solution)/shard_map/reduce_scatter | solution.py:660
  124.2 261.4 %all-reduce.2.cloned.1.call-start = ((), (), s32[]{:S(2)}) async-start(), calls=%async_computation.5 | async-start | bytes 4718592 | tf_op jit(solution)/shard_map/psum | solution.py:735
  124.5 2.6 copy-start.39
  124.5 4.1 copy-start.24
  124.5 5.1 %copy-start.28 = (f32[1024]{0:T(1024)S(1)}, f32[1024]{0:T(1024)}, u32[]{:S(2)}) copy-start(f32[1024]{0:T(1024)} %param.22) | copy-start | bytes 12292
  126.9 13.3 %collective-permute-start.6 = (f32[256,1024]{1,0:T(8,128)}, f32[256,1024]{1,0:T(8,128)}, u32[]{:S(2)}, u32[]{:S(2)}) collective-permute-start(f32[256,1024]{1,0:T(8,128)} %slice.127), channel_id=1, source_target_pairs={{0,4},{4,0},{8,12},{12,8},{16,20},{20,16},{24,28},{28,24},{1,5},{5... | collective-permute-start | bytes 3145736 | tf_op jit(solution)/shard_map/ppermute | solution.py:546
  128.2 26.0 %collective-permute-start.5 = (f32[256,1024]{1,0:T(8,128)}, f32[256,1024]{1,0:T(8,128)}, u32[]{:S(2)}, u32[]{:S(2)}) collective-permute-start(f32[256,1024]{1,0:T(8,128)} %slice.126), channel_id=1, source_target_pairs={{0,4},{4,0},{8,12},{12,8},{16,20},{20,16},{24,28},{28,24},{1,5},{5... | collective-permute-start | bytes 3145736 | tf_op jit(solution)/shard_map/ppermute | solution.py:546
  138.0 49.0 %collective-permute-start.20 = (bf16[256,512]{0,1:T(8,128)(2,1)}, bf16[256,512]{0,1:T(8,128)(2,1)}, u32[]{:S(2)}, u32[]{:S(2)}) collective-permute-start(bf16[256,512]{0,1:T(8,128)(2,1)} %bitcast.139), channel_id=1, source_target_pairs={{0,4},{4,0},{8,12},{12,8},{16,20},{20,16},{24,28},{28,24},{1,5},{5... | collective-permute-start | bytes 786440 | tf_op jit(solution)/shard_map/ppermute | solution.py:546
  140.3 1.6 copy-start.4
  144.4 9.9 %copy-start.40 = (f32[512,1024]{1,0:T(8,128)S(1)}, f32[512,1024]{1,0:T(8,128)}, u32[]{:S(2)}) copy-start(f32[512,1024]{1,0:T(8,128)} %get-tuple-element.40) | copy-start | bytes 6291460
  144.4 9.9 %copy-start.45 = (f32[1024]{0:T(1024)S(1)}, f32[1024]{0:T(1024)}, u32[]{:S(2)}) copy-start(f32[1024]{0:T(1024)} %param.34) | copy-start | bytes 12292
  149.5 7.3 %copy-start.16 = (f32[256,1024]{1,0:T(8,128)}, f32[256,1024]{1,0:T(8,128)S(1)}, u32[]{:S(2)}) copy-start(f32[256,1024]{1,0:T(8,128)S(1)} %get-tuple-element.46.refs_9_) | copy-start | bytes 3145732
  149.5 7.8 %collective-permute-start.7 = (bf16[256,256]{1,0:T(8,128)(2,1)S(1)}, bf16[256,256]{1,0:T(8,128)(2,1)S(1)}, u32[]{:S(2)}, u32[]{:S(2)}) collective-permute-start(bf16[256,256]{1,0:T(8,128)(2,1)S(1)} %get-tuple-element.116), channel_id=1, source_target_pairs={{0,1},{1,0},{2,3},{3,2},{4,5},{5,4},{6,7},{7,6},{8,9},{9,8},{10,11... | collective-permute-start | bytes 393224 | tf_op jit(solution)/shard_map/ppermute | solution.py:546
  151.7 12.9 %collective-permute-start.8 = (bf16[256,256]{1,0:T(8,128)(2,1)S(1)}, bf16[256,256]{1,0:T(8,128)(2,1)S(1)}, u32[]{:S(2)}, u32[]{:S(2)}) collective-permute-start(bf16[256,256]{1,0:T(8,128)(2,1)S(1)} %get-tuple-element.115), channel_id=1, source_target_pairs={{0,2},{1,3},{2,0},{3,1},{4,6},{5,7},{6,4},{7,5},{8,10},{9,11},{10,... | collective-permute-start | bytes 393224 | tf_op jit(solution)/shard_map/ppermute | solution.py:546
  152.5 12.1 %collective-permute-start.9 = (bf16[256,256]{1,0:T(8,128)(2,1)S(1)}, bf16[256,256]{1,0:T(8,128)(2,1)S(1)}, u32[]{:S(2)}, u32[]{:S(2)}) collective-permute-start(bf16[256,256]{1,0:T(8,128)(2,1)S(1)} %get-tuple-element.114), channel_id=1, source_target_pairs={{0,3},{1,2},{2,1},{3,0},{4,7},{5,6},{6,5},{7,4},{8,11},{9,10},{10,... | collective-permute-start | bytes 393224 | tf_op jit(solution)/shard_map/ppermute | solution.py:546
  154.2 10.5 %copy-start.15 = (bf16[4,256,256]{2,1,0:T(8,128)(2,1)S(1)}, bf16[4,256,256]{2,1,0:T(8,128)(2,1)}, u32[]{:S(2)}) copy-start(bf16[4,256,256]{2,1,0:T(8,128)(2,1)} %copy-done.14) | copy-start | bytes 1572868
  154.2 10.5 %copy-start.21 = (s32[1024,1]{1,0:T(8,128)S(1)}, s32[1024,1]{1,0:T(8,128)}, u32[]{:S(2)}) copy-start(s32[1024,1]{1,0:T(8,128)} %copy-done.20) | copy-start | bytes 12292
  154.2 10.5 %copy-start.34 = (bf16[1024,768]{1,0:T(8,128)(2,1)S(1)}, bf16[1024,768]{1,0:T(8,128)(2,1)}, u32[]{:S(2)}) copy-start(bf16[1024,768]{1,0:T(8,128)(2,1)} %copy-done.33) | copy-start | bytes 4718596
  154.2 32.9 %collective-permute-start.21 = (bf16[256,1024]{1,0:T(8,128)(2,1)}, bf16[256,1024]{1,0:T(8,128)(2,1)}, u32[]{:S(2)}, u32[]{:S(2)}) collective-permute-start(bf16[256,1024]{1,0:T(8,128)(2,1)} %get-tuple-element.54), channel_id=1, source_target_pairs={{0,4},{4,0},{8,12},{12,8},{16,20},{20,16},{24,28},{28,24},{1,5},{5... | collective-permute-start | bytes 1572872 | tf_op jit(solution)/shard_map/ppermute | solution.py:546
  186.6 2.0 copy-start.42
  188.6 6.2 %copy-start.10 = (bf16[1024,1024]{1,0:T(8,128)(2,1)S(1)}, bf16[1024,1024]{1,0:T(8,128)(2,1)}, u32[]{:S(2)}) copy-start(bf16[1024,1024]{1,0:T(8,128)(2,1)} %copy-done.9) | copy-start | bytes 6291460
  188.6 6.2 %copy-start.11 = (f32[1024,1]{1,0:T(8,128)S(1)}, f32[1024,1]{1,0:T(8,128)}, u32[]{:S(2)}) copy-start(f32[1024,1]{1,0:T(8,128)} %copy.76.gain) | copy-start | bytes 12292
  188.6 6.1 %copy-start.12 = (f32[1024,1]{1,0:T(8,128)S(1)}, f32[1024,1]{1,0:T(8,128)}, u32[]{:S(2)}) copy-start(f32[1024,1]{1,0:T(8,128)} %copy.77.bias) | copy-start | bytes 12292
  190.3 4.5 %copy-start.36 = (bf16[512,1024]{1,0:T(8,128)(2,1)}, bf16[512,1024]{1,0:T(8,128)(2,1)S(1)}, u32[]{:S(2)}) copy-start(bf16[512,1024]{1,0:T(8,128)(2,1)S(1)} %add_convert_fusion) | copy-start | bytes 3145732
  191.3 15.9 %collective-permute-start.24 = (bf16[128,1024]{1,0:T(8,128)(2,1)}, bf16[128,1024]{1,0:T(8,128)(2,1)S(1)}, u32[]{:S(2)}, u32[]{:S(2)}) collective-permute-start(bf16[128,1024]{1,0:T(8,128)(2,1)} %get-tuple-element.103), channel_id=1, source_target_pairs={{0,24},{4,28},{8,16},{12,20},{16,8},{20,12},{24,0},{28,4},{1,25},{... | collective-permute-start | bytes 786440 | tf_op jit(solution)/shard_map/ppermute | solution.py:546
  193.7 18.5 %collective-permute-start.23 = (bf16[128,1024]{1,0:T(8,128)(2,1)}, bf16[128,1024]{1,0:T(8,128)(2,1)}, u32[]{:S(2)}, u32[]{:S(2)}) collective-permute-start(bf16[128,1024]{1,0:T(8,128)(2,1)} %get-tuple-element.104), channel_id=1, source_target_pairs={{0,16},{4,20},{8,24},{12,28},{16,0},{20,4},{24,8},{28,12},{1,17},{... | collective-permute-start | bytes 786440 | tf_op jit(solution)/shard_map/ppermute | solution.py:546
  194.2 23.3 %collective-permute-start.22 = (bf16[128,1024]{1,0:T(8,128)(2,1)S(1)}, bf16[128,1024]{1,0:T(8,128)(2,1)}, u32[]{:S(2)}, u32[]{:S(2)}) collective-permute-start(bf16[128,1024]{1,0:T(8,128)(2,1)S(1)} %get-tuple-element.102), channel_id=1, source_target_pairs={{0,8},{4,12},{8,0},{12,4},{16,24},{20,28},{24,16},{28,20},{1,9},{5... | collective-permute-start | bytes 786440 | tf_op jit(solution)/shard_map/ppermute | solution.py:546
  194.8 3.0 copy-start.1
  204.5 44.8 %collective-permute-start.13 = (bf16[4,128,896]{1,2,0:T(8,128)(2,1)}, bf16[4,128,896]{1,2,0:T(8,128)(2,1)}, u32[]{:S(2)}, u32[]{:S(2)}) collective-permute-start(bf16[4,128,896]{1,2,0:T(8,128)(2,1)} %bitcast.134), channel_id=1, source_target_pairs={{0,4},{4,0},{8,12},{12,8},{16,20},{20,16},{24,28},{28,24},{1,5},{5... | collective-permute-start | bytes 2752520 | tf_op jit(solution)/shard_map/ppermute | solution.py:546
  207.2 5.0 %copy-start.43 = (bf16[128,1024]{1,0:T(8,128)(2,1)}, bf16[128,1024]{1,0:T(8,128)(2,1)S(1)}, u32[]{:S(2)}) copy-start(bf16[128,1024]{1,0:T(8,128)(2,1)S(1)} %collective-permute-done.24) | copy-start | bytes 786436
  252.8 67.0 %copy-start.17 = (f32[256,1024]{1,0:T(8,128)S(1)}, f32[256,1024]{1,0:T(8,128)}, u32[]{:S(2)}) copy-start(f32[256,1024]{1,0:T(8,128)} %copy-done.16) | copy-start | bytes 3145732
  252.8 14.8 %collective-permute-start.16 = (bf16[128,896]{0,1:T(8,128)(2,1)}, bf16[128,896]{0,1:T(8,128)(2,1)}, u32[]{:S(2)}, u32[]{:S(2)}) collective-permute-start(bf16[128,896]{0,1:T(8,128)(2,1)} %get-tuple-element.110), channel_id=1, source_target_pairs={{0,24},{4,28},{8,16},{12,20},{16,8},{20,12},{24,0},{28,4},{1,25},{... | collective-permute-start | bytes 688136 | tf_op jit(solution)/shard_map/ppermute | solution.py:546
  260.7 7.4 %collective-permute-start.15 = (bf16[128,896]{0,1:T(8,128)(2,1)}, bf16[128,896]{0,1:T(8,128)(2,1)S(1)}, u32[]{:S(2)}, u32[]{:S(2)}) collective-permute-start(bf16[128,896]{0,1:T(8,128)(2,1)} %get-tuple-element.111), channel_id=1, source_target_pairs={{0,16},{4,20},{8,24},{12,28},{16,0},{20,4},{24,8},{28,12},{1,17},{... | collective-permute-start | bytes 688136 | tf_op jit(solution)/shard_map/ppermute | solution.py:546
  262.2 7.0 %collective-permute-start.14 = (bf16[128,896]{0,1:T(8,128)(2,1)}, bf16[128,896]{0,1:T(8,128)(2,1)S(1)}, u32[]{:S(2)}, u32[]{:S(2)}) collective-permute-start(bf16[128,896]{0,1:T(8,128)(2,1)} %get-tuple-element.109), channel_id=1, source_target_pairs={{0,8},{4,12},{8,0},{12,4},{16,24},{20,28},{24,16},{28,20},{1,9},{5... | collective-permute-start | bytes 688136 | tf_op jit(solution)/shard_map/ppermute | solution.py:546
  263.8 37.6 %collective-permute-start.10 = (bf16[256,768]{1,0:T(8,128)(2,1)S(1)}, bf16[256,768]{1,0:T(8,128)(2,1)S(1)}, u32[]{:S(2)}, u32[]{:S(2)}) collective-permute-start(bf16[256,768]{1,0:T(8,128)(2,1)S(1)} %get-tuple-element.97), channel_id=1, source_target_pairs={{0,1},{1,0},{2,3},{3,2},{4,5},{5,4},{6,7},{7,6},{8,9},{9,8},{10,11... | collective-permute-start | bytes 1179656 | tf_op jit(solution)/shard_map/ppermute | solution.py:546
  265.3 43.4 %collective-permute-start.11 = (bf16[256,768]{1,0:T(8,128)(2,1)}, bf16[256,768]{1,0:T(8,128)(2,1)}, u32[]{:S(2)}, u32[]{:S(2)}) collective-permute-start(bf16[256,768]{1,0:T(8,128)(2,1)} %get-tuple-element.96), channel_id=1, source_target_pairs={{0,2},{1,3},{2,0},{3,1},{4,6},{5,7},{6,4},{7,5},{8,10},{9,11},{10,... | collective-permute-start | bytes 1179656 | tf_op jit(solution)/shard_map/ppermute | solution.py:546
  267.7 52.1 %collective-permute-start.12 = (bf16[256,768]{1,0:T(8,128)(2,1)}, bf16[256,768]{1,0:T(8,128)(2,1)}, u32[]{:S(2)}, u32[]{:S(2)}) collective-permute-start(bf16[256,768]{1,0:T(8,128)(2,1)} %get-tuple-element.95), channel_id=1, source_target_pairs={{0,3},{1,2},{2,1},{3,0},{4,7},{5,6},{6,5},{7,4},{8,11},{9,10},{10,... | collective-permute-start | bytes 1179656 | tf_op jit(solution)/shard_map/ppermute | solution.py:546
  271.0 59.3 %collective-permute-start.19 = (bf16[128,896]{0,1:T(8,128)(2,1)}, bf16[128,896]{0,1:T(8,128)(2,1)}, u32[]{:S(2)}, u32[]{:S(2)}) collective-permute-start(bf16[128,896]{0,1:T(8,128)(2,1)} %fusion.8), channel_id=1, source_target_pairs={{0,3},{1,2},{2,1},{3,0},{4,7},{5,6},{6,5},{7,4},{8,11},{9,10},{10,... | collective-permute-start | bytes 688136 | tf_op jit(solution)/shard_map/ppermute | solution.py:546
  274.3 87.3 %collective-permute-start.18 = (bf16[128,896]{0,1:T(8,128)(2,1)}, bf16[128,896]{0,1:T(8,128)(2,1)}, u32[]{:S(2)}, u32[]{:S(2)}) collective-permute-start(bf16[128,896]{0,1:T(8,128)(2,1)} %fusion.8), channel_id=1, source_target_pairs={{0,2},{1,3},{2,0},{3,1},{4,6},{5,7},{6,4},{7,5},{8,10},{9,11},{10,... | collective-permute-start | bytes 688136 | tf_op jit(solution)/shard_map/ppermute | solution.py:546
  301.3 60.3 %collective-permute-start.17 = (bf16[128,896]{0,1:T(8,128)(2,1)}, bf16[128,896]{0,1:T(8,128)(2,1)}, u32[]{:S(2)}, u32[]{:S(2)}) collective-permute-start(bf16[128,896]{0,1:T(8,128)(2,1)} %fusion.8), channel_id=1, source_target_pairs={{0,1},{1,0},{2,3},{3,2},{4,5},{5,4},{6,7},{7,6},{8,9},{9,8},{10,11... | collective-permute-start | bytes 688136 | tf_op jit(solution)/shard_map/ppermute | solution.py:546
  319.8 2.8 copy-start.2
  388.3 10.9 %collective-permute-start.25 = (bf16[128,2048]{0,1:T(8,128)(2,1)}, bf16[128,2048]{0,1:T(8,128)(2,1)}, u32[]{:S(2)}, u32[]{:S(2)}) collective-permute-start(bf16[128,2048]{0,1:T(8,128)(2,1)} %bitcast.62), channel_id=1, source_target_pairs={{0,4},{4,0},{8,12},{12,8},{16,20},{20,16},{24,28},{28,24},{1,5},{5... | collective-permute-start | bytes 1572872 | tf_op jit(solution)/shard_map/ppermute | solution.py:546
  (13 other events, 12.5 us)
Sparse Core Ops, SparseCore 0:
  9.6 48.6 all-gather.1
  123.6 53.2 reduce-scatter.4
  180.1 63.8 reduce-scatter.2
  247.0 138.5 all-reduce.1
